TPU v7x, 256 devices: a whole 4x4x8 slice. The times are simulated.
256 devices in a mesh: fsdp: 32 (over x, y, core), expert: 8 (over z).
Axes of the slice: x: 4, y: 4, z: 8, core: 2. Of those that a mesh axis runs over, the one named last changes fastest.
Arguments:
- grads: bfloat16 [8, 7168, 2048], P(None, ('fsdp', 'expert')), may hold values from -6 to 6
- momentum: float32 [8, 7168, 2048], P(None, ('fsdp', 'expert')), may hold values from -6 to 6
- max_logits: float32 [256, 64], P(('fsdp', 'expert')), may hold values from 4 to 500
- q_weight: bfloat16 [1536, 12288], P('fsdp', 'expert'), may hold values from -6 to 6
- k_weight: bfloat16 [512, 8192], P('fsdp', 'expert'), may hold values from -6 to 6
Outputs:
- new_momentum: float32 [8, 7168, 2048], P(None, ('fsdp', 'expert'))
- step: bfloat16 [8, 7168, 2048], P(None, ('fsdp', 'expert'))
- q_clipped: bfloat16 [1536, 12288], P('fsdp', 'expert')
- k_clipped: bfloat16 [512, 8192], P('fsdp', 'expert')
All inputs are finite; a program needn't handle non-finite values. Where the computation divides by a largest or mean magnitude, that divisor is 1e-20 or more.
Results may differ from a plain program's by a relative error of at most 0.012.
Values may be sent and summed in bfloat16 or wider, within the bound.
No kernel may reach another device: no remote copies, remote signals or barrier semaphores. Data moves between devices by JAX's collectives and lax.ppermute only.
A program may use at most 128 MiB of HBM per device.

v0:
```python
import math

import jax
import jax.numpy as jnp
from jax import lax
from jax.experimental import pallas as pl
from jax.experimental.pallas import tpu as pltpu
from jax.sharding import Mesh, PartitionSpec as P

D = 7168
FF = 2048
NOPE = 128
ROPE = 64

decay_rate = 0.9
linear_coef = 3.4445
cubic_coef = -4.775
quintic_coef = 2.0315
clip_limit = 100.0
rms_match = 0.2

NX, NY, NC, NZ = 4, 4, 2, 8
PLANE = ("x", "y", "c")
BLK = 128
NB = FF // BLK
HALF = FF // 2
BAND = (NB // 2 + 1) * BLK
PADROWS = 32
KROWS = NZ * PADROWS
CUT = 512
TAIL = 384
PACKED = FF + (FF // CUT) * TAIL
WIDTH = PACKED + BLK
EXTRA = 16
QUARTER = 2 * BLK

MASS = pl.BlockSpec(memory_space=pltpu.VMEM)
SCALARS = pl.BlockSpec(memory_space=pltpu.SMEM)
FAR = pl.BlockSpec(memory_space=pl.ANY)


def room(mib):
    return pltpu.CompilerParams(vmem_limit_bytes=mib * 1024 * 1024)


def low_rows(value):
    return lax.broadcasted_iota(jnp.int32, value.shape, 1) < 4


def pack(tiles):
    t0, t1, t2, t3 = tiles
    e2, e3 = t2[:, :, TAIL:], t3[:, :, TAIL:]
    moved = jnp.concatenate([pltpu.roll(e2, 4, 1), e2, pltpu.roll(e3, 4, 1)], axis=2)
    last = t3[:, :, :TAIL]
    last = jnp.where(low_rows(last), last, moved)
    head = jnp.concatenate([t0, t1], axis=1)
    tail = jnp.concatenate([t2[:, :, :TAIL], last], axis=1)
    return head.astype(jnp.bfloat16), tail.astype(jnp.bfloat16)


def unpack(head, tail):
    head, tail = head.astype(jnp.float32), tail.astype(jnp.float32)
    t2, last = tail[:, :8], tail[:, 8:]
    m0, m1, m2 = last[:, :, :BLK], last[:, :, BLK : 2 * BLK], last[:, :, 2 * BLK :]
    e2 = jnp.where(low_rows(m0), pltpu.roll(m0, 4, 1), m1)
    e3 = pltpu.roll(m2, 4, 1)
    t2 = jnp.concatenate([t2, e2], axis=2)
    t3 = jnp.concatenate([last, e3], axis=2)
    t3 = jnp.where(low_rows(t3), t3, 0.0)
    return head[:, :8], head[:, 8:], t2, t3


def split_terms(value):
    high = value.astype(jnp.bfloat16).astype(jnp.float32)
    rest = value - high
    middle = rest.astype(jnp.bfloat16).astype(jnp.float32)
    row = lax.broadcasted_iota(jnp.int32, (EXTRA, BLK), 0)
    tile = jnp.where(row == 0, high, jnp.where(row == 1, middle, jnp.where(row == 2, rest - middle, 0.0)))
    return tile.astype(jnp.bfloat16)


def largest(tiles):
    best = None
    for tile in tiles:
        tile = tile.astype(jnp.float32)
        value = tile[0:1] + tile[1:2] + tile[2:3]
        best = value if best is None else jnp.maximum(best, value)
    return best


def head_columns(n):
    return pl.ds(pl.multiple_of(n * CUT, CUT), CUT)


def tail_columns(n):
    return pl.ds(pl.multiple_of(FF + n * TAIL, BLK), TAIL)


def direction_kernel(logits_ref, grads_ref, momentum_ref, *refs):
    outs, (grads_buf, momentum_buf, packed_ref, grads_sem, momentum_sem) = refs[:NZ], refs[NZ:]
    z = lax.axis_index("z")
    copies = []
    for n in range(FF // CUT):
        columns = pl.ds(n * CUT, CUT)
        pair = (
            pltpu.make_async_copy(momentum_ref.at[:, :, columns], momentum_buf.at[n], momentum_sem.at[n]),
            pltpu.make_async_copy(grads_ref.at[:, :, columns], grads_buf.at[n], grads_sem.at[n]),
        )
        for copy in pair:
            copy.start()
        copies.append(pair)
    for n in range(FF // CUT):
        for copy in copies[n]:
            copy.wait()
        grads = grads_buf[n].astype(jnp.float32)
        direction = grads + decay_rate * (decay_rate * momentum_buf[n] + grads)
        rows, mats, columns = direction.shape
        direction = jnp.concatenate([direction, jnp.zeros((PADROWS - rows, mats, columns), jnp.float32)], axis=0)
        head, tail = pack([jnp.swapaxes(direction[8 * t : 8 * t + 8], 0, 1) for t in range(4)])
        packed_ref[:, :, head_columns(n)] = head
        packed_ref[:, :, tail_columns(n)] = tail
    logits = logits_ref[...]
    terms = split_terms(jnp.concatenate([logits, jnp.zeros((1, BLK - logits.shape[1]), jnp.float32)], axis=1))
    for d in range(NZ):
        outs[d][:, :PACKED] = packed_ref[(z + d) % NZ]
        outs[d][:, PACKED:] = terms


def find_direction(logits, grads, momentum):
    rows, mats = grads.shape[:2]
    cuts = FF // CUT
    return pl.pallas_call(
        direction_kernel,
        out_shape=[jax.ShapeDtypeStruct((16, WIDTH), jnp.bfloat16)] * NZ,
        in_specs=[MASS] + [FAR] * 2,
        out_specs=[MASS] * NZ,
        scratch_shapes=[
            pltpu.VMEM((cuts, rows, mats, CUT), jnp.bfloat16),
            pltpu.VMEM((cuts, rows, mats, CUT), jnp.float32),
            pltpu.VMEM((mats, 16, PACKED), jnp.bfloat16),
            pltpu.SemaphoreType.DMA((cuts,)),
            pltpu.SemaphoreType.DMA((cuts,)),
        ],
        compiler_params=room(60),
        name="find_direction",
    )(logits, grads, momentum)


def momentum_kernel(grads_ref, momentum_ref, out_ref, grads_buf, momentum_buf, in_sem, out_sem):
    copies = []
    for n in range(FF // CUT):
        columns = pl.ds(n * CUT, CUT)
        trio = (
            pltpu.make_async_copy(momentum_ref.at[:, :, columns], momentum_buf.at[n], in_sem.at[0, n]),
            pltpu.make_async_copy(grads_ref.at[:, :, columns], grads_buf.at[n], in_sem.at[1, n]),
            pltpu.make_async_copy(momentum_buf.at[n], out_ref.at[:, :, columns], out_sem.at[n]),
        )
        trio[0].start()
        trio[1].start()
        copies.append(trio)
    for n in range(FF // CUT):
        copies[n][0].wait()
        copies[n][1].wait()
        momentum_buf[n] = decay_rate * momentum_buf[n] + grads_buf[n].astype(jnp.float32)
        copies[n][2].start()
    for trio in copies:
        trio[2].wait()


def add_momentum(grads, momentum):
    rows, mats = grads.shape[:2]
    cuts = FF // CUT
    return pl.pallas_call(
        momentum_kernel,
        out_shape=jax.ShapeDtypeStruct(grads.shape, jnp.float32),
        in_specs=[FAR] * 2,
        out_specs=FAR,
        scratch_shapes=[
            pltpu.VMEM((cuts, rows, mats, CUT), jnp.bfloat16),
            pltpu.VMEM((cuts, rows, mats, CUT), jnp.float32),
            pltpu.SemaphoreType.DMA((2, cuts)),
            pltpu.SemaphoreType.DMA((cuts,)),
        ],
        compiler_params=room(58),
        name="add_momentum",
    )(grads, momentum)


def spread_kernel(place_ref, *refs):
    blocks, (out_ref, packed_ref, rows_ref, sem) = refs[:NZ], refs[NZ:]
    z = place_ref[3]
    for d in range(NZ):
        packed_ref[(z + d) % NZ] = blocks[d][...]
    copies = []
    for n in range(FF // CUT):
        tiles = unpack(packed_ref[:, :, head_columns(n)], packed_ref[:, :, tail_columns(n)])
        rows = jnp.concatenate([jnp.swapaxes(t, 0, 1) for t in tiles], axis=0)
        rows_ref[n] = rows[: out_ref.shape[0]].astype(jnp.bfloat16)
        copy = pltpu.make_async_copy(rows_ref.at[n], out_ref.at[:, :, pl.ds(n * CUT, CUT)], sem.at[n])
        copy.start()
        copies.append(copy)
    for copy in copies:
        copy.wait()


def spread_step(place, blocks, rows):
    cuts = FF // CUT
    return pl.pallas_call(
        spread_kernel,
        out_shape=jax.ShapeDtypeStruct((rows, NZ, FF), jnp.bfloat16),
        in_specs=[SCALARS] + [MASS] * NZ,
        out_specs=pl.BlockSpec(memory_space=pl.ANY),
        scratch_shapes=[
            pltpu.VMEM((NZ, 16, PACKED), jnp.bfloat16),
            pltpu.VMEM((cuts, rows, NZ, CUT), jnp.bfloat16),
            pltpu.SemaphoreType.DMA((cuts,)),
        ],
        compiler_params=room(16),
        name="spread_step",
    )(place, *blocks)


def gram_kernel(place_ref, *refs):
    blocks, shares, (x_ref, rows_ref, band_ref) = refs[: 2 * NZ], refs[2 * NZ : 2 * NZ + 4], refs[2 * NZ + 4 :]
    along, core = place_ref[0], place_ref[2]
    for n in range(FF // CUT):
        source = (n + 2 * core) % 4
        columns = pl.ds(n * CUT, CUT)
        for half in range(2):
            packed = blocks[half * NZ : (half + 1) * NZ]
            head = jnp.stack([block[:, head_columns(source)] for block in packed])
            tail = jnp.stack([block[:, tail_columns(source)] for block in packed])
            tiles = unpack(head, tail)
            rows = jnp.concatenate(tiles, axis=1).reshape(KROWS, CUT).astype(jnp.bfloat16)
            rows_ref[pl.ds(half * KROWS, KROWS), columns] = rows
            if half == 0:
                x_ref[:, columns] = rows
    for q in range(4):
        left = rows_ref[:, pl.ds(q * QUARTER, QUARTER)]
        right = rows_ref[:, pl.ds(q * QUARTER, BAND + BLK)]
        product = lax.dot_general(
            left, right, (((0,), (0,)), ((), ())), preferred_element_type=jnp.float32
        ).astype(jnp.bfloat16)
        for sub in range(2):
            band_ref[pl.ds(q * QUARTER + sub * BLK, BLK), :] = product[
                sub * BLK : (sub + 1) * BLK, sub * BLK : sub * BLK + BAND
            ]
    terms = split_terms(largest([block[:, PACKED:] for block in blocks]))
    for d in range(4):
        shares[d][:QUARTER] = band_ref[quarter_rows(along + d), :]
        put_terms(shares[d], QUARTER, terms)


def put_terms(ref, row, terms):
    ref[pl.ds(row, EXTRA), :BLK] = terms
    ref[pl.ds(row, EXTRA), BLK:] = jnp.zeros((EXTRA, BAND - BLK), jnp.bfloat16)


def quarter_rows(q, start=0):
    return pl.ds(pl.multiple_of(start + (q % 4) * QUARTER, QUARTER), QUARTER)


def gram_band(place, blocks):
    return pl.pallas_call(
        gram_kernel,
        out_shape=[jax.ShapeDtypeStruct((QUARTER + EXTRA, BAND), jnp.bfloat16)] * 4
        + [jax.ShapeDtypeStruct((KROWS, FF), jnp.bfloat16)],
        in_specs=[SCALARS] + [MASS] * (2 * NZ),
        out_specs=[MASS] * 5,
        scratch_shapes=[
            pltpu.VMEM((2 * KROWS, FF), jnp.bfloat16),
            pltpu.VMEM((HALF, BAND), jnp.bfloat16),
        ],
        compiler_params=room(28),
        name="gram_band",
    )(place, *blocks)


def quarter_kernel(*refs):
    parts, outs = refs[:4], refs[4:]
    for half in range(2):
        rows = pl.ds(half * BLK, BLK)
        total = sum(part[rows, :].astype(jnp.float32) for part in parts)
        outs[half][:BLK] = total.astype(jnp.bfloat16)
    put_terms(outs[0], BLK, split_terms(largest([part[QUARTER:, :BLK] for part in parts])))


HALVES = [
    jax.ShapeDtypeStruct((BLK + EXTRA, BAND), jnp.bfloat16),
    jax.ShapeDtypeStruct((BLK, BAND), jnp.bfloat16),
]


def sum_quarter(parts):
    return pl.pallas_call(
        quarter_kernel,
        out_shape=HALVES,
        in_specs=[MASS] * 4,
        out_specs=[MASS] * 2,
        compiler_params=room(16),
        name="sum_quarter",
    )(*parts)


def pair_kernel(*refs):
    mine, came, outs = refs[:2], refs[2:4], refs[4:]
    for half in range(2):
        total = mine[half][:BLK].astype(jnp.float32) + came[half][:BLK].astype(jnp.float32)
        outs[half][:BLK] = total.astype(jnp.bfloat16)
    put_terms(outs[0], BLK, split_terms(largest([mine[0][BLK:, :BLK], came[0][BLK:, :BLK]])))


def add_pairs(mine, came):
    return pl.pallas_call(
        pair_kernel,
        out_shape=HALVES,
        in_specs=[MASS] * 4,
        out_specs=[MASS] * 2,
        compiler_params=room(16),
        name="add_pairs",
    )(*mine, *came)


def join_kernel(*refs):
    mine, came, (out_ref, peak_ref) = refs[:2], refs[2:4], refs[4:]
    for half in range(2):
        total = mine[half][:BLK].astype(jnp.float32) + came[half][:BLK].astype(jnp.float32)
        out_ref[pl.ds(half * BLK, BLK), :] = total.astype(jnp.bfloat16)
    peak_ref[...] = largest([mine[0][BLK:, :BLK], came[0][BLK:, :BLK]])


def join_pairs(mine, came):
    return pl.pallas_call(
        join_kernel,
        out_shape=[
            jax.ShapeDtypeStruct((QUARTER, BAND), jnp.bfloat16),
            jax.ShapeDtypeStruct((1, BLK), jnp.float32),
        ],
        in_specs=[MASS] * 4,
        out_specs=[MASS] * 2,
        compiler_params=room(16),
        name="join_pairs",
    )(*mine, *came)


def step_kernel(place_ref, x_ref, *refs):
    pieces = refs[:8]
    outs, (band_ref, gram_ref, first_ref, round_ref) = refs[8 : 8 + NZ], refs[8 + NZ :]
    core = place_ref[2]
    for side in range(2):
        for d in range(4):
            rows = quarter_rows(place_ref[side] + (4 - d), side * HALF)
            band_ref[rows, :] = pieces[side * 4 + d][...]
    for i in range(NB):
        block = band_ref[pl.ds(i * BLK, BLK), :]
        turned = block[:, BLK : BAND - BLK].T
        for d in range(NB // 2 + 1):
            j = (i + d) % NB
            gram_ref[pl.ds(i * BLK, BLK), pl.ds(j * BLK, BLK)] = block[:, d * BLK : (d + 1) * BLK]
            if 1 <= d < NB // 2:
                gram_ref[pl.ds(j * BLK, BLK), pl.ds(i * BLK, BLK)] = turned[(d - 1) * BLK : d * BLK]

    ones = jnp.ones((16, FF), jnp.bfloat16)
    bound = jnp.zeros((1, 1), jnp.float32)
    for n in range(FF // CUT):
        columns = pl.ds(n * CUT, CUT)
        gram = gram_ref[:, columns]
        first_ref[:, columns] = jnp.dot(x_ref[...], gram, preferred_element_type=jnp.float32)
        sums = jnp.dot(ones, jnp.abs(gram), preferred_element_type=jnp.float32)
        bound = jnp.maximum(bound, jnp.max(sums[:8], keepdims=True))
    inverse = 1.0 / bound
    scale = rms_match * math.sqrt(max(D, FF)) / jnp.sqrt(bound)
    for n in range(FF // CUT):
        columns = pl.ds(n * CUT, CUT)
        first = first_ref[:, columns] * inverse
        round_ref[:, columns] = first.astype(jnp.bfloat16)
        first_ref[:, columns] = linear_coef * x_ref[:, columns].astype(jnp.float32) + cubic_coef * first
    for n in range(FF // CUT):
        columns = pl.ds(n * CUT, CUT)
        second = jnp.dot(round_ref[...], gram_ref[:, columns], preferred_element_type=jnp.float32) * inverse
        step = scale * (first_ref[:, columns] + quintic_coef * second)
        step = step.reshape(NZ, PADROWS, CUT)
        head, tail = pack([step[:, 8 * t : 8 * t + 8] for t in range(4)])
        target = (n + 2 * core) % 4
        for d in range(NZ):
            outs[d][:, head_columns(target)] = head[d]
            outs[d][:, tail_columns(target)] = tail[d]


def finish(place, mine, pieces):
    return pl.pallas_call(
        step_kernel,
        out_shape=[jax.ShapeDtypeStruct((16, PACKED), jnp.bfloat16)] * NZ,
        in_specs=[SCALARS] + [MASS] * 9,
        out_specs=[MASS] * NZ,
        scratch_shapes=[
            pltpu.VMEM((FF, BAND), jnp.bfloat16),
            pltpu.VMEM((FF, FF), jnp.bfloat16),
            pltpu.VMEM((KROWS, FF), jnp.float32),
            pltpu.VMEM((KROWS, FF), jnp.bfloat16),
        ],
        compiler_params=room(40),
        name="finish",
    )(place, mine, *pieces)


def place_of(x, y, core):
    return (x * NY + y) * NC + core


def permutation(step):
    pairs = []
    for x in range(NX):
        for y in range(NY):
            for core in range(NC):
                mine = (x, y) if core == 0 else (y, x)
                to = step(*mine)
                to = to if core == 0 else to[::-1]
                pairs.append((place_of(x, y, core), place_of(*to, core)))
    return pairs


def send_along(value, by):
    return lax.ppermute(value, PLANE, permutation(lambda along, across: ((along + by) % 4, across)))


LINKS = ((1, 0, 3, 2), (3, 2, 1, 0))


def trade_across(values, first):
    links = (LINKS[first], LINKS[1 - first])
    return [
        lax.ppermute(value, PLANE, permutation(lambda along, across, link=link: (along, link[across])))
        for value, link in zip(values, links)
    ]


def collect(own, sends):
    came = {d: send_along(sends(d), d) for d in (2, 1, 3)}
    return [own, came[1], came[2], came[3]]


def swap_cores(value):
    return lax.ppermute(value, "c", [(0, 1), (1, 0)])


def trade_planes(blocks, sign):
    came = [blocks[0]] + [None] * (NZ - 1)
    for d in (4, 3, 5, 2, 6, 1, 7):
        came[d] = lax.ppermute(blocks[d], "z", [(i, (i + sign * d) % NZ) for i in range(NZ)])
    return came


def body(grads, momentum, max_logits, q_weight, k_weight):
    x, y, core = lax.axis_index("x"), lax.axis_index("y"), lax.axis_index("c")
    along, across = jnp.where(core == 0, x, y), jnp.where(core == 0, y, x)
    place = jnp.stack([along, across, core, lax.axis_index("z")]).astype(jnp.int32)
    grads, momentum = jnp.swapaxes(grads, 0, 1), jnp.swapaxes(momentum, 0, 1)
    blocks = find_direction(max_logits, grads, momentum)
    owned = trade_planes(blocks, 1)
    other = [None] * NZ
    for d in (0, 4, 3, 5, 2, 6, 1, 7):
        other[d] = swap_cores(owned[d])
    *shares, mine = gram_band(place, owned + other)
    shares[0], grads_again, momentum = lax.optimization_barrier((shares[0], grads, momentum))
    parts = collect(shares[0], lambda d: shares[d])
    new_momentum = add_momentum(grads_again, momentum)
    parts[0], new_momentum = lax.optimization_barrier((parts[0], new_momentum))
    held = sum_quarter(parts)
    held = add_pairs(held, trade_across(held, 0))
    held, peak = join_pairs(held, trade_across(held, 1))
    pieces = collect(held, lambda d: held)
    pieces[0], pieces[2] = lax.optimization_barrier((pieces[0], pieces[2]))
    other = [swap_cores(piece) for piece in pieces]
    step = list(finish(place, mine, pieces + other))
    step[0], peak, q_weight, k_weight = lax.optimization_barrier((step[0], peak, q_weight, k_weight))
    step = trade_planes(step, -1)
    peak = peak[0, : max_logits.shape[1]]

    gamma = jnp.minimum(1.0, clip_limit / peak)
    root = jnp.sqrt(gamma)
    local_heads = k_weight.shape[1] // NOPE
    first_head = lax.axis_index("z") * local_heads
    gamma_mine = lax.dynamic_slice_in_dim(gamma, first_head, local_heads)
    root_mine = lax.dynamic_slice_in_dim(root, first_head, local_heads)
    q_factor = jnp.concatenate(
        [
            jnp.broadcast_to(root_mine[:, None], (local_heads, NOPE)),
            jnp.broadcast_to(gamma_mine[:, None], (local_heads, ROPE)),
        ],
        axis=1,
    )
    q_view = q_weight.reshape(q_weight.shape[0], local_heads, NOPE + ROPE).astype(jnp.float32)
    q_clipped = (q_view * q_factor[None]).astype(jnp.bfloat16).reshape(q_weight.shape)
    k_view = k_weight.reshape(k_weight.shape[0], local_heads, NOPE).astype(jnp.float32)
    k_clipped = (k_view * root_mine[None, :, None]).astype(jnp.bfloat16).reshape(k_weight.shape)
    step[0], q_clipped, k_clipped = lax.optimization_barrier((step[0], q_clipped, k_clipped))
    step = jnp.swapaxes(spread_step(place, step, grads.shape[0]), 0, 1)
    new_momentum = jnp.swapaxes(new_momentum, 0, 1)
    return (new_momentum, step, q_clipped, k_clipped)


def solution(mesh):
    split = Mesh(mesh.devices.reshape(NX, NY, NC, NZ), ("x", "y", "c", "z"))
    rows = P(None, ("x", "y", "c", "z"), None)
    heads = P(("x", "y", "c"), "z")
    return jax.shard_map(
        body,
        mesh=split,
        in_specs=(rows, rows, P(("x", "y", "c", "z"), None), heads, heads),
        out_specs=(rows, rows, heads, heads),
        check_vma=False,
    )
```

profile of v0, /device:TPU:2, one launch (start us, length us, event | category | flops | bytes accessed | tf_op | source)
XLA Modules:
  0.0 150.1 jit_solution(12356291332685668389)
XLA Ops:
  0.6 3.6 %find_direction.1 = (bf16[16,3712]{1,0:T(8,128)(2,1)}, bf16[16,3712]{1,0:T(8,128)(2,1)}, bf16[16,3712]{1,0:T(8,128)(2,1)}, bf16[16,3712]{1,0:T(8,128)(2,1)}, bf1...) custom-call(f32[1,64]{1,0:T(1,128)} %logits_ref.1, ...), custom_call_target="tpu_custom_call" | custom-call | tf_op jit(solution)/shard_map/find_direction/pallas_call | solution.py:132
  4.3 2.0 %collective-permute-start = (bf16[16,3712]{1,0:T(8,128)(2,1)}, bf16[16,3712]{1,0:T(8,128)(2,1)S(1)}, u32[]{:S(2)}, u32[]{:S(2)}) collective-permute-start(bf16[16,3712]{1,0:T(8,128)(2,1)} %get-tuple-element.46), channel_id=1, source_target_pairs={{0,1},{1,2},{2,3},{3,4},{4,5},{5,6},{6,7},{7,0},{8,9},{9,10},{10,1... | collective-permute-start | bytes 356360 | tf_op jit(solution)/shard_map/ppermute | solution.py:450
  6.3 3.3 %collective-permute-start.1 = (bf16[16,3712]{1,0:T(8,128)(2,1)}, bf16[16,3712]{1,0:T(8,128)(2,1)S(1)}, u32[]{:S(2)}, u32[]{:S(2)}) collective-permute-start(bf16[16,3712]{1,0:T(8,128)(2,1)} %get-tuple-element.47), channel_id=1, source_target_pairs={{0,2},{1,3},{2,4},{3,5},{4,6},{5,7},{6,0},{7,1},{8,10},{9,11},{10,... | collective-permute-start | bytes 356360 | tf_op jit(solution)/shard_map/ppermute | solution.py:450
  9.6 4.0 %collective-permute-start.2 = (bf16[16,3712]{1,0:T(8,128)(2,1)}, bf16[16,3712]{1,0:T(8,128)(2,1)S(1)}, u32[]{:S(2)}, u32[]{:S(2)}) collective-permute-start(bf16[16,3712]{1,0:T(8,128)(2,1)} %get-tuple-element.48), channel_id=1, source_target_pairs={{0,3},{1,4},{2,5},{3,6},{4,7},{5,0},{6,1},{7,2},{8,11},{9,12},{10,... | collective-permute-start | bytes 356360 | tf_op jit(solution)/shard_map/ppermute | solution.py:450
  14.1 4.9 %collective-permute-start.4 = (bf16[16,3712]{1,0:T(8,128)(2,1)}, bf16[16,3712]{1,0:T(8,128)(2,1)S(1)}, u32[]{:S(2)}, u32[]{:S(2)}) collective-permute-start(bf16[16,3712]{1,0:T(8,128)(2,1)} %get-tuple-element.50), channel_id=1, source_target_pairs={{0,5},{1,6},{2,7},{3,0},{4,1},{5,2},{6,3},{7,4},{8,13},{9,14},{10,... | collective-permute-start | bytes 356360 | tf_op jit(solution)/shard_map/ppermute | solution.py:450
  19.1 2.7 %collective-permute-start.5 = (bf16[16,3712]{1,0:T(8,128)(2,1)}, bf16[16,3712]{1,0:T(8,128)(2,1)S(1)}, u32[]{:S(2)}, u32[]{:S(2)}) collective-permute-start(bf16[16,3712]{1,0:T(8,128)(2,1)} %get-tuple-element.51), channel_id=1, source_target_pairs={{0,6},{1,7},{2,0},{3,1},{4,2},{5,3},{6,4},{7,5},{8,14},{9,15},{10,... | collective-permute-start | bytes 356360 | tf_op jit(solution)/shard_map/ppermute | solution.py:450
  22.5 3.2 %collective-permute-start.6 = (bf16[16,3712]{1,0:T(8,128)(2,1)}, bf16[16,3712]{1,0:T(8,128)(2,1)S(1)}, u32[]{:S(2)}, u32[]{:S(2)}) collective-permute-start(bf16[16,3712]{1,0:T(8,128)(2,1)} %get-tuple-element.52), channel_id=1, source_target_pairs={{0,7},{1,0},{2,1},{3,2},{4,3},{5,4},{6,5},{7,6},{8,15},{9,8},{10,9... | collective-permute-start | bytes 356360 | tf_op jit(solution)/shard_map/ppermute | solution.py:450
  25.7 4.1 %collective-permute-done.2.refs_3_ = bf16[16,3712]{1,0:T(8,128)(2,1)S(1)} collective-permute-done((bf16[16,3712]{1,0:T(8,128)(2,1)}, bf16[16,3712]{1,0:T(8,128)(2,1)S(1)}, u32[]{:S(2)}, u32[]{:S(2)}) %collective-permute-start.2) | collective-permute-done | bytes 118816 | tf_op jit(solution)/shard_map/ppermute | solution.py:450
  30.4 3.7 %collective-permute-done.4.refs_5_ = bf16[16,3712]{1,0:T(8,128)(2,1)S(1)} collective-permute-done((bf16[16,3712]{1,0:T(8,128)(2,1)}, bf16[16,3712]{1,0:T(8,128)(2,1)S(1)}, u32[]{:S(2)}, u32[]{:S(2)}) %collective-permute-start.4) | collective-permute-done | bytes 118816 | tf_op jit(solution)/shard_map/ppermute | solution.py:450
  34.1 1.7 %collective-permute-done.5.refs_6_ = bf16[16,3712]{1,0:T(8,128)(2,1)S(1)} collective-permute-done((bf16[16,3712]{1,0:T(8,128)(2,1)}, bf16[16,3712]{1,0:T(8,128)(2,1)S(1)}, u32[]{:S(2)}, u32[]{:S(2)}) %collective-permute-start.5) | collective-permute-done | bytes 118816 | tf_op jit(solution)/shard_map/ppermute | solution.py:450
  39.8 3.3 %gram_band.1 = (bf16[272,1152]{1,0:T(8,128)(2,1)S(1)}, bf16[272,1152]{1,0:T(8,128)(2,1)}, bf16[272,1152]{1,0:T(8,128)(2,1)}, bf16[272,1152]{1,0:T(8,128)(2,1)S(1)}, bf16[256,2048]{1,0:T(8,128)(2,1)S(1)}) custom-call(s32[4]{0:T(128)S(1)} %pad_add_fusion.place_ref, bf16[16,3712]{1,0:T(8,128)(2,1)S(1)} %copy-done, ...), custom_call_target="tpu_custom_call" | custom-call | tf_op jit(solution)/shard_map/gram_band/pallas_call | solution.py:264
  45.8 2.2 %collective-permute-start.17 = (bf16[272,1152]{1,0:T(8,128)(2,1)S(1)}, bf16[272,1152]{1,0:T(8,128)(2,1)S(1)}, u32[]{:S(2)}, u32[]{:S(2)}) collective-permute-start(bf16[272,1152]{1,0:T(8,128)(2,1)S(1)} %get-tuple-element.62), channel_id=1, source_target_pairs={{0,192},{8,56},{16,208},{24,8},{32,224},{40,24},{48,240},{56,40},{... | collective-permute-start | bytes 1880072 | tf_op jit(solution)/shard_map/ppermute | solution.py:424
  47.9 2.7 %add_momentum.1 = f32[28,8,2048]{2,1,0:T(8,128)} custom-call(bf16[28,8,2048]{2,1,0:T(8,128)(2,1)} %bitcast.17, f32[28,8,2048]{2,1,0:T(8,128)} %bitcast.15), custom_call_target="tpu_custom_call" | custom-call | tf_op jit(solution)/shard_map/add_momentum/pallas_call | solution.py:173
  50.6 3.1 %collective-permute-done.15.refs_1_ = bf16[272,1152]{1,0:T(8,128)(2,1)S(1)} collective-permute-done((bf16[272,1152]{1,0:T(8,128)(2,1)}, bf16[272,1152]{1,0:T(8,128)(2,1)S(1)}, u32[]{:S(2)}, u32[]{:S(2)}) %collective-permute-start.15) | collective-permute-done | bytes 626720 | tf_op jit(solution)/shard_map/ppermute | solution.py:424
  53.6 3.1 %collective-permute-done.16.refs_2_ = bf16[272,1152]{1,0:T(8,128)(2,1)S(1)} collective-permute-done((bf16[272,1152]{1,0:T(8,128)(2,1)}, bf16[272,1152]{1,0:T(8,128)(2,1)S(1)}, u32[]{:S(2)}, u32[]{:S(2)}) %collective-permute-start.16) | collective-permute-done | bytes 626720 | tf_op jit(solution)/shard_map/ppermute | solution.py:424
  56.8 6.0 %collective-permute-done.17.refs_3_ = bf16[272,1152]{1,0:T(8,128)(2,1)S(1)} collective-permute-done((bf16[272,1152]{1,0:T(8,128)(2,1)S(1)}, bf16[272,1152]{1,0:T(8,128)(2,1)S(1)}, u32[]{:S(2)}, u32[]{:S(2)}) %collective-permute-start.17) | collective-permute-done | bytes 626720 | tf_op jit(solution)/shard_map/ppermute | solution.py:424
  64.7 2.2 %collective-permute-start.19 = (bf16[128,1152]{1,0:T(8,128)(2,1)S(1)}, bf16[128,1152]{1,0:T(8,128)(2,1)S(1)}, u32[]{:S(2)}, u32[]{:S(2)}) collective-permute-start(bf16[128,1152]{1,0:T(8,128)(2,1)S(1)} %get-tuple-element.64.refs_1_), channel_id=1, source_target_pairs={{0,48},{8,200},{16,32},{24,216},{32,16},{40,232},{48,0},{56,248},{... | collective-permute-start | bytes 884744 | tf_op jit(solution)/shard_map/ppermute | solution.py:433
  66.9 5.8 %collective-permute-done.19.refs_3_ = bf16[128,1152]{1,0:T(8,128)(2,1)S(1)} collective-permute-done((bf16[128,1152]{1,0:T(8,128)(2,1)S(1)}, bf16[128,1152]{1,0:T(8,128)(2,1)S(1)}, u32[]{:S(2)}, u32[]{:S(2)}) %collective-permute-start.19) | collective-permute-done | bytes 294944 | tf_op jit(solution)/shard_map/ppermute | solution.py:433
  72.8 2.3 %collective-permute-start.20 = (bf16[144,1152]{1,0:T(8,128)(2,1)S(1)}, bf16[144,1152]{1,0:T(8,128)(2,1)S(1)}, u32[]{:S(2)}, u32[]{:S(2)}) collective-permute-start(bf16[144,1152]{1,0:T(8,128)(2,1)S(1)} %get-tuple-element.65.refs_0_), channel_id=1, source_target_pairs={{0,48},{8,200},{16,32},{24,216},{32,16},{40,232},{48,0},{56,248},{... | collective-permute-start | bytes 995336 | tf_op jit(solution)/shard_map/ppermute | solution.py:433
  75.1 7.6 %collective-permute-done.21.refs_3_ = bf16[128,1152]{1,0:T(8,128)(2,1)S(1)} collective-permute-done((bf16[128,1152]{1,0:T(8,128)(2,1)S(1)}, bf16[128,1152]{1,0:T(8,128)(2,1)S(1)}, u32[]{:S(2)}, u32[]{:S(2)}) %collective-permute-start.21) | collective-permute-done | bytes 294944 | tf_op jit(solution)/shard_map/ppermute | solution.py:433
  83.8 3.1 %collective-permute-start.24 = (bf16[256,1152]{1,0:T(8,128)(2,1)S(1)}, bf16[256,1152]{1,0:T(8,128)(2,1)S(1)}, u32[]{:S(2)}, u32[]{:S(2)}) collective-permute-start(bf16[256,1152]{1,0:T(8,128)(2,1)S(1)} %get-tuple-element.68.refs_0_), channel_id=1, source_target_pairs={{0,192},{8,56},{16,208},{24,8},{32,224},{40,24},{48,240},{56,40},{... | collective-permute-start | bytes 1769480 | tf_op jit(solution)/shard_map/ppermute | solution.py:424
  86.9 7.5 %collective-permute-done.22.refs_2_ = bf16[256,1152]{1,0:T(8,128)(2,1)S(1)} collective-permute-done((bf16[256,1152]{1,0:T(8,128)(2,1)S(1)}, bf16[256,1152]{1,0:T(8,128)(2,1)S(1)}, u32[]{:S(2)}, u32[]{:S(2)}) %collective-permute-start.22) | collective-permute-done | bytes 589856 | tf_op jit(solution)/shard_map/ppermute | solution.py:424
  94.4 5.5 %collective-permute-done.24.refs_3_ = bf16[256,1152]{1,0:T(8,128)(2,1)S(1)} collective-permute-done((bf16[256,1152]{1,0:T(8,128)(2,1)S(1)}, bf16[256,1152]{1,0:T(8,128)(2,1)S(1)}, u32[]{:S(2)}, u32[]{:S(2)}) %collective-permute-start.24) | collective-permute-done | bytes 589856 | tf_op jit(solution)/shard_map/ppermute | solution.py:424
  104.1 8.4 %finish.1 = (bf16[16,3584]{1,0:T(8,128)(2,1)S(1)}, bf16[16,3584]{1,0:T(8,128)(2,1)S(1)}, bf16[16,3584]{1,0:T(8,128)(2,1)S(1)}, bf16[16,3584]{1,0:T(8,128)(2,1)S(...) custom-call(s32[4]{0:T(128)S(1)} %pad_add_fusion.place_ref, ...), custom_call_target="tpu_custom_call" | custom-call | tf_op jit(solution)/shard_map/finish/pallas_call | solution.py:391
  117.3 2.7 %collective-permute-start.29 = (bf16[16,3584]{1,0:T(8,128)(2,1)}, bf16[16,3584]{1,0:T(8,128)(2,1)S(1)}, u32[]{:S(2)}, u32[]{:S(2)}) collective-permute-start(bf16[16,3584]{1,0:T(8,128)(2,1)} %copy-done.7), channel_id=1, source_target_pairs={{0,7},{1,0},{2,1},{3,2},{4,3},{5,4},{6,5},{7,6},{8,15},{9,8},{10,9... | collective-permute-start | bytes 344072 | tf_op jit(solution)/shard_map/ppermute | solution.py:450
  120.5 3.8 %collective-permute-start.31 = (bf16[16,3584]{1,0:T(8,128)(2,1)}, bf16[16,3584]{1,0:T(8,128)(2,1)S(1)}, u32[]{:S(2)}, u32[]{:S(2)}) collective-permute-start(bf16[16,3584]{1,0:T(8,128)(2,1)} %copy-done.5), channel_id=1, source_target_pairs={{0,5},{1,6},{2,7},{3,0},{4,1},{5,2},{6,3},{7,4},{8,13},{9,14},{10,... | collective-permute-start | bytes 344072 | tf_op jit(solution)/shard_map/ppermute | solution.py:450
  126.1 3.0 %collective-permute-start.33 = (bf16[16,3584]{1,0:T(8,128)(2,1)}, bf16[16,3584]{1,0:T(8,128)(2,1)S(1)}, u32[]{:S(2)}, u32[]{:S(2)}) collective-permute-start(bf16[16,3584]{1,0:T(8,128)(2,1)} %copy-done.3), channel_id=1, source_target_pairs={{0,3},{1,4},{2,5},{3,6},{4,7},{5,0},{6,1},{7,2},{8,11},{9,12},{10,... | collective-permute-start | bytes 344072 | tf_op jit(solution)/shard_map/ppermute | solution.py:450
  130.8 2.4 %collective-permute-start.34 = (bf16[16,3584]{1,0:T(8,128)(2,1)}, bf16[16,3584]{1,0:T(8,128)(2,1)S(1)}, u32[]{:S(2)}, u32[]{:S(2)}) collective-permute-start(bf16[16,3584]{1,0:T(8,128)(2,1)} %copy-done.2), channel_id=1, source_target_pairs={{0,2},{1,3},{2,4},{3,5},{4,6},{5,7},{6,0},{7,1},{8,10},{9,11},{10,... | collective-permute-start | bytes 344072 | tf_op jit(solution)/shard_map/ppermute | solution.py:450
  133.1 1.9 %collective-permute-done.30.refs_2_ = bf16[16,3584]{1,0:T(8,128)(2,1)S(1)} collective-permute-done((bf16[16,3584]{1,0:T(8,128)(2,1)}, bf16[16,3584]{1,0:T(8,128)(2,1)S(1)}, u32[]{:S(2)}, u32[]{:S(2)}) %collective-permute-start.30) | collective-permute-done | bytes 114720 | tf_op jit(solution)/shard_map/ppermute | solution.py:450
  138.2 6.0 %collective-permute-done.33.refs_5_ = bf16[16,3584]{1,0:T(8,128)(2,1)S(1)} collective-permute-done((bf16[16,3584]{1,0:T(8,128)(2,1)}, bf16[16,3584]{1,0:T(8,128)(2,1)S(1)}, u32[]{:S(2)}, u32[]{:S(2)}) %collective-permute-start.33) | collective-permute-done | bytes 114720 | tf_op jit(solution)/shard_map/ppermute | solution.py:450
  144.2 3.9 %collective-permute-done.35.refs_7_ = bf16[16,3584]{1,0:T(8,128)(2,1)S(1)} collective-permute-done((bf16[16,3584]{1,0:T(8,128)(2,1)}, bf16[16,3584]{1,0:T(8,128)(2,1)S(1)}, u32[]{:S(2)}, u32[]{:S(2)}) %collective-permute-start.35) | collective-permute-done | bytes 114720 | tf_op jit(solution)/shard_map/ppermute | solution.py:450
  148.1 1.8 %spread_step.1 = bf16[28,8,2048]{2,1,0:T(8,128)(2,1)} custom-call(s32[4]{0:T(128)S(1)} %pad_add_fusion.place_ref, bf16[16,3584]{1,0:T(8,128)(2,1)S(1)} %get-tuple-element.76.refs_0_, bf16[16,3584]{1,0:T(8,128)(2,1)S(1)} %collective-permute-done.29.refs_1_, bf16[16,3584]{1,0:T(8,128)(2,1)S(1)} %collective-permute-done.30.refs_2_, ...), custom_call_target="tpu_custom_call" | custom-call | tf_op jit(solution)/shard_map/spread_step/pallas_call | solution.py:208
  (74 shorter events, 27.5 us)
Async XLA Ops:
  4.3 14.8 %collective-permute-start = (bf16[16,3712]{1,0:T(8,128)(2,1)}, bf16[16,3712]{1,0:T(8,128)(2,1)S(1)}, u32[]{:S(2)}, u32[]{:S(2)}) collective-permute-start(bf16[16,3712]{1,0:T(8,128)(2,1)} %get-tuple-element.46), channel_id=1, source_target_pairs={{0,1},{1,2},{2,3},{3,4},{4,5},{5,6},{6,7},{7,0},{8,9},{9,10},{10,1... | collective-permute-start | bytes 356360 | tf_op jit(solution)/shard_map/ppermute | solution.py:450
  6.3 16.2 %collective-permute-start.1 = (bf16[16,3712]{1,0:T(8,128)(2,1)}, bf16[16,3712]{1,0:T(8,128)(2,1)S(1)}, u32[]{:S(2)}, u32[]{:S(2)}) collective-permute-start(bf16[16,3712]{1,0:T(8,128)(2,1)} %get-tuple-element.47), channel_id=1, source_target_pairs={{0,2},{1,3},{2,4},{3,5},{4,6},{5,7},{6,0},{7,1},{8,10},{9,11},{10,... | collective-permute-start | bytes 356360 | tf_op jit(solution)/shard_map/ppermute | solution.py:450
  9.6 20.3 %collective-permute-start.2 = (bf16[16,3712]{1,0:T(8,128)(2,1)}, bf16[16,3712]{1,0:T(8,128)(2,1)S(1)}, u32[]{:S(2)}, u32[]{:S(2)}) collective-permute-start(bf16[16,3712]{1,0:T(8,128)(2,1)} %get-tuple-element.48), channel_id=1, source_target_pairs={{0,3},{1,4},{2,5},{3,6},{4,7},{5,0},{6,1},{7,2},{8,11},{9,12},{10,... | collective-permute-start | bytes 356360 | tf_op jit(solution)/shard_map/ppermute | solution.py:450
  13.6 16.3 %collective-permute-start.3 = (bf16[16,3712]{1,0:T(8,128)(2,1)}, bf16[16,3712]{1,0:T(8,128)(2,1)S(1)}, u32[]{:S(2)}, u32[]{:S(2)}) collective-permute-start(bf16[16,3712]{1,0:T(8,128)(2,1)} %get-tuple-element.49), channel_id=1, source_target_pairs={{0,4},{1,5},{2,6},{3,7},{4,0},{5,1},{6,2},{7,3},{8,12},{9,13},{10,... | collective-permute-start | bytes 356360 | tf_op jit(solution)/shard_map/ppermute | solution.py:450
  14.1 19.9 %collective-permute-start.4 = (bf16[16,3712]{1,0:T(8,128)(2,1)}, bf16[16,3712]{1,0:T(8,128)(2,1)S(1)}, u32[]{:S(2)}, u32[]{:S(2)}) collective-permute-start(bf16[16,3712]{1,0:T(8,128)(2,1)} %get-tuple-element.50), channel_id=1, source_target_pairs={{0,5},{1,6},{2,7},{3,0},{4,1},{5,2},{6,3},{7,4},{8,13},{9,14},{10,... | collective-permute-start | bytes 356360 | tf_op jit(solution)/shard_map/ppermute | solution.py:450
  19.1 16.7 %collective-permute-start.5 = (bf16[16,3712]{1,0:T(8,128)(2,1)}, bf16[16,3712]{1,0:T(8,128)(2,1)S(1)}, u32[]{:S(2)}, u32[]{:S(2)}) collective-permute-start(bf16[16,3712]{1,0:T(8,128)(2,1)} %get-tuple-element.51), channel_id=1, source_target_pairs={{0,6},{1,7},{2,0},{3,1},{4,2},{5,3},{6,4},{7,5},{8,14},{9,15},{10,... | collective-permute-start | bytes 356360 | tf_op jit(solution)/shard_map/ppermute | solution.py:450
  22.5 14.4 %collective-permute-start.6 = (bf16[16,3712]{1,0:T(8,128)(2,1)}, bf16[16,3712]{1,0:T(8,128)(2,1)S(1)}, u32[]{:S(2)}, u32[]{:S(2)}) collective-permute-start(bf16[16,3712]{1,0:T(8,128)(2,1)} %get-tuple-element.52), channel_id=1, source_target_pairs={{0,7},{1,0},{2,1},{3,2},{4,3},{5,4},{6,5},{7,6},{8,15},{9,8},{10,9... | collective-permute-start | bytes 356360 | tf_op jit(solution)/shard_map/ppermute | solution.py:450
  29.9 7.0 %collective-permute-start.7 = (bf16[16,3712]{1,0:T(8,128)(2,1)}, bf16[16,3712]{1,0:T(8,128)(2,1)S(1)}, u32[]{:S(2)}, u32[]{:S(2)}) collective-permute-start(bf16[16,3712]{1,0:T(8,128)(2,1)} %get-tuple-element.45.refs_0_), channel_id=1, source_target_pairs={{0,8},{8,0},{1,9},{9,1},{2,10},{10,2},{3,11},{11,3},{4,12},{12,4},... | collective-permute-start | bytes 356360 | tf_op jit(solution)/shard_map/ppermute | solution.py:444
  29.9 7.6 %collective-permute-start.8 = (bf16[16,3712]{1,0:T(8,128)(2,1)S(1)}, bf16[16,3712]{1,0:T(8,128)(2,1)S(1)}, u32[]{:S(2)}, u32[]{:S(2)}) collective-permute-start(bf16[16,3712]{1,0:T(8,128)(2,1)S(1)} %collective-permute-done.refs_1_), channel_id=1, source_target_pairs={{0,8},{8,0},{1,9},{9,1},{2,10},{10,2},{3,11},{11,3},{4,12},{12,4},... | collective-permute-start | bytes 356360 | tf_op jit(solution)/shard_map/ppermute | solution.py:444
  34.1 3.4 %collective-permute-start.9 = (bf16[16,3712]{1,0:T(8,128)(2,1)S(1)}, bf16[16,3712]{1,0:T(8,128)(2,1)S(1)}, u32[]{:S(2)}, u32[]{:S(2)}) collective-permute-start(bf16[16,3712]{1,0:T(8,128)(2,1)S(1)} %collective-permute-done.1.refs_2_), channel_id=1, source_target_pairs={{0,8},{8,0},{1,9},{9,1},{2,10},{10,2},{3,11},{11,3},{4,12},{12,4},... | collective-permute-start | bytes 356360 | tf_op jit(solution)/shard_map/ppermute | solution.py:444
  35.8 2.2 %collective-permute-start.10 = (bf16[16,3712]{1,0:T(8,128)(2,1)S(1)}, bf16[16,3712]{1,0:T(8,128)(2,1)S(1)}, u32[]{:S(2)}, u32[]{:S(2)}) collective-permute-start(bf16[16,3712]{1,0:T(8,128)(2,1)S(1)} %collective-permute-done.2.refs_3_), channel_id=1, source_target_pairs={{0,8},{8,0},{1,9},{9,1},{2,10},{10,2},{3,11},{11,3},{4,12},{12,4},... | collective-permute-start | bytes 356360 | tf_op jit(solution)/shard_map/ppermute | solution.py:444
  43.2 10.5 %collective-permute-start.15 = (bf16[272,1152]{1,0:T(8,128)(2,1)}, bf16[272,1152]{1,0:T(8,128)(2,1)S(1)}, u32[]{:S(2)}, u32[]{:S(2)}) collective-permute-start(bf16[272,1152]{1,0:T(8,128)(2,1)} %get-tuple-element.60), channel_id=1, source_target_pairs={{0,64},{8,24},{16,80},{24,40},{32,96},{40,56},{48,112},{56,8},{64,... | collective-permute-start | bytes 1880072 | tf_op jit(solution)/shard_map/ppermute | solution.py:424
  44.7 12.1 %collective-permute-start.16 = (bf16[272,1152]{1,0:T(8,128)(2,1)}, bf16[272,1152]{1,0:T(8,128)(2,1)S(1)}, u32[]{:S(2)}, u32[]{:S(2)}) collective-permute-start(bf16[272,1152]{1,0:T(8,128)(2,1)} %get-tuple-element.61), channel_id=1, source_target_pairs={{0,128},{8,40},{16,144},{24,56},{32,160},{40,8},{48,176},{56,24},{... | collective-permute-start | bytes 1880072 | tf_op jit(solution)/shard_map/ppermute | solution.py:424
  45.8 17.0 %collective-permute-start.17 = (bf16[272,1152]{1,0:T(8,128)(2,1)S(1)}, bf16[272,1152]{1,0:T(8,128)(2,1)S(1)}, u32[]{:S(2)}, u32[]{:S(2)}) collective-permute-start(bf16[272,1152]{1,0:T(8,128)(2,1)S(1)} %get-tuple-element.62), channel_id=1, source_target_pairs={{0,192},{8,56},{16,208},{24,8},{32,224},{40,24},{48,240},{56,40},{... | collective-permute-start | bytes 1880072 | tf_op jit(solution)/shard_map/ppermute | solution.py:424
  63.1 9.6 %collective-permute-start.18 = (bf16[144,1152]{1,0:T(8,128)(2,1)S(1)}, bf16[144,1152]{1,0:T(8,128)(2,1)S(1)}, u32[]{:S(2)}, u32[]{:S(2)}) collective-permute-start(bf16[144,1152]{1,0:T(8,128)(2,1)S(1)} %get-tuple-element.63.refs_0_), channel_id=1, source_target_pairs={{0,16},{8,72},{16,0},{24,88},{32,48},{40,104},{48,32},{56,120},{64... | collective-permute-start | bytes 995336 | tf_op jit(solution)/shard_map/ppermute | solution.py:433
  64.7 7.9 %collective-permute-start.19 = (bf16[128,1152]{1,0:T(8,128)(2,1)S(1)}, bf16[128,1152]{1,0:T(8,128)(2,1)S(1)}, u32[]{:S(2)}, u32[]{:S(2)}) collective-permute-start(bf16[128,1152]{1,0:T(8,128)(2,1)S(1)} %get-tuple-element.64.refs_1_), channel_id=1, source_target_pairs={{0,48},{8,200},{16,32},{24,216},{32,16},{40,232},{48,0},{56,248},{... | collective-permute-start | bytes 884744 | tf_op jit(solution)/shard_map/ppermute | solution.py:433
  72.8 9.9 %collective-permute-start.20 = (bf16[144,1152]{1,0:T(8,128)(2,1)S(1)}, bf16[144,1152]{1,0:T(8,128)(2,1)S(1)}, u32[]{:S(2)}, u32[]{:S(2)}) collective-permute-start(bf16[144,1152]{1,0:T(8,128)(2,1)S(1)} %get-tuple-element.65.refs_0_), channel_id=1, source_target_pairs={{0,48},{8,200},{16,32},{24,216},{32,16},{40,232},{48,0},{56,248},{... | collective-permute-start | bytes 995336 | tf_op jit(solution)/shard_map/ppermute | solution.py:433
  75.1 7.6 %collective-permute-start.21 = (bf16[128,1152]{1,0:T(8,128)(2,1)S(1)}, bf16[128,1152]{1,0:T(8,128)(2,1)S(1)}, u32[]{:S(2)}, u32[]{:S(2)}) collective-permute-start(bf16[128,1152]{1,0:T(8,128)(2,1)S(1)} %get-tuple-element.66.refs_1_), channel_id=1, source_target_pairs={{0,16},{8,72},{16,0},{24,88},{32,48},{40,104},{48,32},{56,120},{64... | collective-permute-start | bytes 884744 | tf_op jit(solution)/shard_map/ppermute | solution.py:433
  82.9 11.6 %collective-permute-start.22 = (bf16[256,1152]{1,0:T(8,128)(2,1)S(1)}, bf16[256,1152]{1,0:T(8,128)(2,1)S(1)}, u32[]{:S(2)}, u32[]{:S(2)}) collective-permute-start(bf16[256,1152]{1,0:T(8,128)(2,1)S(1)} %get-tuple-element.68.refs_0_), channel_id=1, source_target_pairs={{0,128},{8,40},{16,144},{24,56},{32,160},{40,8},{48,176},{56,24},{... | collective-permute-start | bytes 1769480 | tf_op jit(solution)/shard_map/ppermute | solution.py:424
  83.8 16.2 %collective-permute-start.24 = (bf16[256,1152]{1,0:T(8,128)(2,1)S(1)}, bf16[256,1152]{1,0:T(8,128)(2,1)S(1)}, u32[]{:S(2)}, u32[]{:S(2)}) collective-permute-start(bf16[256,1152]{1,0:T(8,128)(2,1)S(1)} %get-tuple-element.68.refs_0_), channel_id=1, source_target_pairs={{0,192},{8,56},{16,208},{24,8},{32,224},{40,24},{48,240},{56,40},{... | collective-permute-start | bytes 1769480 | tf_op jit(solution)/shard_map/ppermute | solution.py:424
  86.9 14.2 %collective-permute-start.23 = (bf16[256,1152]{1,0:T(8,128)(2,1)S(1)}, bf16[256,1152]{1,0:T(8,128)(2,1)S(1)}, u32[]{:S(2)}, u32[]{:S(2)}) collective-permute-start(bf16[256,1152]{1,0:T(8,128)(2,1)S(1)} %get-tuple-element.68.refs_0_), channel_id=1, source_target_pairs={{0,64},{8,24},{16,80},{24,40},{32,96},{40,56},{48,112},{56,8},{64,... | collective-permute-start | bytes 1769480 | tf_op jit(solution)/shard_map/ppermute | solution.py:424
  94.4 8.8 %collective-permute-start.25 = (bf16[256,1152]{1,0:T(8,128)(2,1)S(1)}, bf16[256,1152]{1,0:T(8,128)(2,1)}, u32[]{:S(2)}, u32[]{:S(2)}) collective-permute-start(bf16[256,1152]{1,0:T(8,128)(2,1)S(1)} %get-tuple-element.68.refs_0_), channel_id=1, source_target_pairs={{0,8},{8,0},{1,9},{9,1},{2,10},{10,2},{3,11},{11,3},{4,12},{12,4},... | collective-permute-start | bytes 1769480 | tf_op jit(solution)/shard_map/ppermute | solution.py:444
  100.0 2.1 %collective-permute-start.28 = (bf16[256,1152]{1,0:T(8,128)(2,1)S(1)}, bf16[256,1152]{1,0:T(8,128)(2,1)}, u32[]{:S(2)}, u32[]{:S(2)}) collective-permute-start(bf16[256,1152]{1,0:T(8,128)(2,1)S(1)} %collective-permute-done.24.refs_3_), channel_id=1, source_target_pairs={{0,8},{8,0},{1,9},{9,1},{2,10},{10,2},{3,11},{11,3},{4,12},{12,4},... | collective-permute-start | bytes 1769480 | tf_op jit(solution)/shard_map/ppermute | solution.py:444
  101.1 2.1 %collective-permute-start.26 = (bf16[256,1152]{1,0:T(8,128)(2,1)S(1)}, bf16[256,1152]{1,0:T(8,128)(2,1)}, u32[]{:S(2)}, u32[]{:S(2)}) collective-permute-start(bf16[256,1152]{1,0:T(8,128)(2,1)S(1)} %collective-permute-done.23.refs_1_), channel_id=1, source_target_pairs={{0,8},{8,0},{1,9},{9,1},{2,10},{10,2},{3,11},{11,3},{4,12},{12,4},... | collective-permute-start | bytes 1769480 | tf_op jit(solution)/shard_map/ppermute | solution.py:444
  101.1 3.0 %collective-permute-start.27 = (bf16[256,1152]{1,0:T(8,128)(2,1)S(1)}, bf16[256,1152]{1,0:T(8,128)(2,1)}, u32[]{:S(2)}, u32[]{:S(2)}) collective-permute-start(bf16[256,1152]{1,0:T(8,128)(2,1)S(1)} %collective-permute-done.22.refs_2_), channel_id=1, source_target_pairs={{0,8},{8,0},{1,9},{9,1},{2,10},{10,2},{3,11},{11,3},{4,12},{12,4},... | collective-permute-start | bytes 1769480 | tf_op jit(solution)/shard_map/ppermute | solution.py:444
  117.3 13.5 %collective-permute-start.29 = (bf16[16,3584]{1,0:T(8,128)(2,1)}, bf16[16,3584]{1,0:T(8,128)(2,1)S(1)}, u32[]{:S(2)}, u32[]{:S(2)}) collective-permute-start(bf16[16,3584]{1,0:T(8,128)(2,1)} %copy-done.7), channel_id=1, source_target_pairs={{0,7},{1,0},{2,1},{3,2},{4,3},{5,4},{6,5},{7,6},{8,15},{9,8},{10,9... | collective-permute-start | bytes 344072 | tf_op jit(solution)/shard_map/ppermute | solution.py:450
  120.0 15.1 %collective-permute-start.30 = (bf16[16,3584]{1,0:T(8,128)(2,1)}, bf16[16,3584]{1,0:T(8,128)(2,1)S(1)}, u32[]{:S(2)}, u32[]{:S(2)}) collective-permute-start(bf16[16,3584]{1,0:T(8,128)(2,1)} %copy-done.6), channel_id=1, source_target_pairs={{0,6},{1,7},{2,0},{3,1},{4,2},{5,3},{6,4},{7,5},{8,14},{9,15},{10,... | collective-permute-start | bytes 344072 | tf_op jit(solution)/shard_map/ppermute | solution.py:450
  120.5 16.0 %collective-permute-start.31 = (bf16[16,3584]{1,0:T(8,128)(2,1)}, bf16[16,3584]{1,0:T(8,128)(2,1)S(1)}, u32[]{:S(2)}, u32[]{:S(2)}) collective-permute-start(bf16[16,3584]{1,0:T(8,128)(2,1)} %copy-done.5), channel_id=1, source_target_pairs={{0,5},{1,6},{2,7},{3,0},{4,1},{5,2},{6,3},{7,4},{8,13},{9,14},{10,... | collective-permute-start | bytes 344072 | tf_op jit(solution)/shard_map/ppermute | solution.py:450
  124.4 13.8 %collective-permute-start.32 = (bf16[16,3584]{1,0:T(8,128)(2,1)}, bf16[16,3584]{1,0:T(8,128)(2,1)S(1)}, u32[]{:S(2)}, u32[]{:S(2)}) collective-permute-start(bf16[16,3584]{1,0:T(8,128)(2,1)} %copy-done.4), channel_id=1, source_target_pairs={{0,4},{1,5},{2,6},{3,7},{4,0},{5,1},{6,2},{7,3},{8,12},{9,13},{10,... | collective-permute-start | bytes 344072 | tf_op jit(solution)/shard_map/ppermute | solution.py:450
  126.1 18.1 %collective-permute-start.33 = (bf16[16,3584]{1,0:T(8,128)(2,1)}, bf16[16,3584]{1,0:T(8,128)(2,1)S(1)}, u32[]{:S(2)}, u32[]{:S(2)}) collective-permute-start(bf16[16,3584]{1,0:T(8,128)(2,1)} %copy-done.3), channel_id=1, source_target_pairs={{0,3},{1,4},{2,5},{3,6},{4,7},{5,0},{6,1},{7,2},{8,11},{9,12},{10,... | collective-permute-start | bytes 344072 | tf_op jit(solution)/shard_map/ppermute | solution.py:450
  130.8 13.4 %collective-permute-start.34 = (bf16[16,3584]{1,0:T(8,128)(2,1)}, bf16[16,3584]{1,0:T(8,128)(2,1)S(1)}, u32[]{:S(2)}, u32[]{:S(2)}) collective-permute-start(bf16[16,3584]{1,0:T(8,128)(2,1)} %copy-done.2), channel_id=1, source_target_pairs={{0,2},{1,3},{2,4},{3,5},{4,6},{5,7},{6,0},{7,1},{8,10},{9,11},{10,... | collective-permute-start | bytes 344072 | tf_op jit(solution)/shard_map/ppermute | solution.py:450
  135.1 13.0 %collective-permute-start.35 = (bf16[16,3584]{1,0:T(8,128)(2,1)}, bf16[16,3584]{1,0:T(8,128)(2,1)S(1)}, u32[]{:S(2)}, u32[]{:S(2)}) collective-permute-start(bf16[16,3584]{1,0:T(8,128)(2,1)} %copy-done.1), channel_id=1, source_target_pairs={{0,1},{1,2},{2,3},{3,4},{4,5},{5,6},{6,7},{7,0},{8,9},{9,10},{10,1... | collective-permute-start | bytes 344072 | tf_op jit(solution)/shard_map/ppermute | solution.py:450
  (12 other events, 11.0 us)
where the time goes:
time: 151 us; the launch traced here: 150 us
  waiting for transfers between devices  68.1 us (45%)
  starting transfers between devices  51.8 us (34%)
  Pallas kernels  20.5 us (14%)
  local copies, waits for them, and re-layouts  5.75 us (4%)
  other arithmetic  3.07 us (2%)
    ppermute x14, starting transfers between devices, trade_planes(): lax.ppermute(blocks[d], 'z', [(i, (i + sign * d) % NZ) for i in range(NZ)])  34.8 us
    ppermute x6, waiting for transfers between devices, send_along(): lax.ppermute(value, PLANE, permutation(lambda along, across: ((along + by...  26.4 us
    ppermute x14, waiting for transfers between devices, trade_planes(): lax.ppermute(blocks[d], 'z', [(i, (i + sign * d) % NZ) for i in range(NZ)])  25 us
    ppermute x4, waiting for transfers between devices, trade_across(): lax.ppermute(value, PLANE, permutation(lambda along, across, link=link: (...  13.4 us
    ppermute x6, starting transfers between devices, send_along(): lax.ppermute(value, PLANE, permutation(lambda along, across: ((along + by...  8.79 us
    pallas_call x1, Pallas kernels, finish(): pl.pallas_call(step_kernel, out_shape=[jax.ShapeDtypeStruct((16, PACKED),...  8.39 us
    ppermute x4, starting transfers between devices, trade_across(): lax.ppermute(value, PLANE, permutation(lambda along, across, link=link: (...  6.11 us
    unnamed x16, local copies, waits for them, and re-layouts  5.39 us
  transfers between devices with their start and end apart: 36, of which 24 were waited for; matrix products, arithmetic and copies ran while one was open for 2% of the time, Pallas kernels for 2%

commit v1 on v0

--- a/solution.py
+++ b/solution.py
@@ -35,8 +35,12 @@
 QUARTER = 2 * BLK
 
 MASS = pl.BlockSpec(memory_space=pltpu.VMEM)
-SCALARS = pl.BlockSpec(memory_space=pltpu.SMEM)
 FAR = pl.BlockSpec(memory_space=pl.ANY)
+
+
+def own_place():
+    x, y, core = lax.axis_index("x"), lax.axis_index("y"), lax.axis_index("c")
+    return jnp.where(core == 0, x, y), jnp.where(core == 0, y, x), core
 
 
 def room(mib):
@@ -141,7 +145,7 @@
             pltpu.SemaphoreType.DMA((cuts,)),
             pltpu.SemaphoreType.DMA((cuts,)),
         ],
-        compiler_params=room(60),
+        compiler_params=room(53),
         name="find_direction",
     )(logits, grads, momentum)
 
@@ -181,14 +185,14 @@
             pltpu.SemaphoreType.DMA((2, cuts)),
             pltpu.SemaphoreType.DMA((cuts,)),
         ],
-        compiler_params=room(58),
+        compiler_params=room(53),
         name="add_momentum",
     )(grads, momentum)
 
 
-def spread_kernel(place_ref, *refs):
+def spread_kernel(*refs):
     blocks, (out_ref, packed_ref, rows_ref, sem) = refs[:NZ], refs[NZ:]
-    z = place_ref[3]
+    z = lax.axis_index("z")
     for d in range(NZ):
         packed_ref[(z + d) % NZ] = blocks[d][...]
     copies = []
@@ -203,12 +207,12 @@
         copy.wait()
 
 
-def spread_step(place, blocks, rows):
+def spread_step(blocks, rows):
     cuts = FF // CUT
     return pl.pallas_call(
         spread_kernel,
         out_shape=jax.ShapeDtypeStruct((rows, NZ, FF), jnp.bfloat16),
-        in_specs=[SCALARS] + [MASS] * NZ,
+        in_specs=[MASS] * NZ,
         out_specs=pl.BlockSpec(memory_space=pl.ANY),
         scratch_shapes=[
             pltpu.VMEM((NZ, 16, PACKED), jnp.bfloat16),
@@ -217,12 +221,12 @@
         ],
         compiler_params=room(16),
         name="spread_step",
-    )(place, *blocks)
-
-
-def gram_kernel(place_ref, *refs):
+    )(*blocks)
+
+
+def gram_kernel(*refs):
     blocks, shares, (x_ref, rows_ref, band_ref) = refs[: 2 * NZ], refs[2 * NZ : 2 * NZ + 4], refs[2 * NZ + 4 :]
-    along, core = place_ref[0], place_ref[2]
+    along, _, core = own_place()
     for n in range(FF // CUT):
         source = (n + 2 * core) % 4
         columns = pl.ds(n * CUT, CUT)
@@ -260,12 +264,12 @@
     return pl.ds(pl.multiple_of(start + (q % 4) * QUARTER, QUARTER), QUARTER)
 
 
-def gram_band(place, blocks):
+def gram_band(blocks):
     return pl.pallas_call(
         gram_kernel,
         out_shape=[jax.ShapeDtypeStruct((QUARTER + EXTRA, BAND), jnp.bfloat16)] * 4
         + [jax.ShapeDtypeStruct((KROWS, FF), jnp.bfloat16)],
-        in_specs=[SCALARS] + [MASS] * (2 * NZ),
+        in_specs=[MASS] * (2 * NZ),
         out_specs=[MASS] * 5,
         scratch_shapes=[
             pltpu.VMEM((2 * KROWS, FF), jnp.bfloat16),
@@ -273,7 +277,7 @@
         ],
         compiler_params=room(28),
         name="gram_band",
-    )(place, *blocks)
+    )(*blocks)
 
 
 def quarter_kernel(*refs):
@@ -343,13 +347,13 @@
     )(*mine, *came)
 
 
-def step_kernel(place_ref, x_ref, *refs):
+def step_kernel(x_ref, *refs):
     pieces = refs[:8]
     outs, (band_ref, gram_ref, first_ref, round_ref) = refs[8 : 8 + NZ], refs[8 + NZ :]
-    core = place_ref[2]
+    *places, core = own_place()
     for side in range(2):
         for d in range(4):
-            rows = quarter_rows(place_ref[side] + (4 - d), side * HALF)
+            rows = quarter_rows(places[side] + (4 - d), side * HALF)
             band_ref[rows, :] = pieces[side * 4 + d][...]
     for i in range(NB):
         block = band_ref[pl.ds(i * BLK, BLK), :]
@@ -387,11 +391,11 @@
             outs[d][:, tail_columns(target)] = tail[d]
 
 
-def finish(place, mine, pieces):
+def finish(mine, pieces):
     return pl.pallas_call(
         step_kernel,
         out_shape=[jax.ShapeDtypeStruct((16, PACKED), jnp.bfloat16)] * NZ,
-        in_specs=[SCALARS] + [MASS] * 9,
+        in_specs=[MASS] * 9,
         out_specs=[MASS] * NZ,
         scratch_shapes=[
             pltpu.VMEM((FF, BAND), jnp.bfloat16),
@@ -399,9 +403,37 @@
             pltpu.VMEM((KROWS, FF), jnp.float32),
             pltpu.VMEM((KROWS, FF), jnp.bfloat16),
         ],
-        compiler_params=room(40),
+        compiler_params=room(28),
         name="finish",
-    )(place, mine, *pieces)
+    )(mine, *pieces)
+
+
+def clip_kernel(peak_ref, q_ref, k_ref, q_out, k_out):
+    z = lax.axis_index("z")
+    gamma = jnp.minimum(1.0, clip_limit / peak_ref[...])
+    square = (BLK, BLK)
+    diagonal = lax.broadcasted_iota(jnp.int32, square, 0) == lax.broadcasted_iota(jnp.int32, square, 1)
+    gamma = jnp.sum(jnp.where(diagonal, jnp.broadcast_to(gamma, square), 0.0), axis=1, keepdims=True)
+    root = jnp.sqrt(gamma)
+    for source, out, width in ((q_ref, q_out, NOPE + ROPE), (k_ref, k_out, NOPE)):
+        columns = source.shape[1]
+        column = lax.broadcasted_iota(jnp.int32, (BLK, columns), 1)
+        head = column // width
+        chosen = lax.broadcasted_iota(jnp.int32, (BLK, columns), 0) == head + z * (columns // width)
+        value = jnp.where(column - head * width < NOPE, root, gamma)
+        factor = jnp.sum(jnp.where(chosen, value, 0.0), axis=0, keepdims=True)
+        out[...] = (source[...].astype(jnp.float32) * factor).astype(jnp.bfloat16)
+
+
+def clip(peak, q_weight, k_weight):
+    return pl.pallas_call(
+        clip_kernel,
+        out_shape=[jax.ShapeDtypeStruct(weight.shape, jnp.bfloat16) for weight in (q_weight, k_weight)],
+        in_specs=[MASS] * 3,
+        out_specs=[MASS] * 2,
+        compiler_params=room(16),
+        name="clip",
+    )(peak, q_weight, k_weight)
 
 
 def place_of(x, y, core):
@@ -435,8 +467,8 @@
     ]
 
 
-def collect(own, sends):
-    came = {d: send_along(sends(d), d) for d in (2, 1, 3)}
+def collect(own, sends, order):
+    came = {d: send_along(sends(d), d) for d in order}
     return [own, came[1], came[2], came[3]]
 
 
@@ -452,52 +484,28 @@
 
 
 def body(grads, momentum, max_logits, q_weight, k_weight):
-    x, y, core = lax.axis_index("x"), lax.axis_index("y"), lax.axis_index("c")
-    along, across = jnp.where(core == 0, x, y), jnp.where(core == 0, y, x)
-    place = jnp.stack([along, across, core, lax.axis_index("z")]).astype(jnp.int32)
     grads, momentum = jnp.swapaxes(grads, 0, 1), jnp.swapaxes(momentum, 0, 1)
     blocks = find_direction(max_logits, grads, momentum)
     owned = trade_planes(blocks, 1)
     other = [None] * NZ
     for d in (0, 4, 3, 5, 2, 6, 1, 7):
         other[d] = swap_cores(owned[d])
-    *shares, mine = gram_band(place, owned + other)
+    *shares, mine = gram_band(owned + other)
     shares[0], grads_again, momentum = lax.optimization_barrier((shares[0], grads, momentum))
-    parts = collect(shares[0], lambda d: shares[d])
+    parts = collect(shares[0], lambda d: shares[d], (2, 1, 3))
     new_momentum = add_momentum(grads_again, momentum)
     parts[0], new_momentum = lax.optimization_barrier((parts[0], new_momentum))
     held = sum_quarter(parts)
     held = add_pairs(held, trade_across(held, 0))
     held, peak = join_pairs(held, trade_across(held, 1))
-    pieces = collect(held, lambda d: held)
-    pieces[0], pieces[2] = lax.optimization_barrier((pieces[0], pieces[2]))
+    pieces = collect(held, lambda d: held, (1, 3, 2))
+    q_clipped, k_clipped = clip(peak, q_weight, k_weight)
+    pieces[0], pieces[1], q_clipped, k_clipped = lax.optimization_barrier((pieces[0], pieces[1], q_clipped, k_clipped))
     other = [swap_cores(piece) for piece in pieces]
-    step = list(finish(place, mine, pieces + other))
-    step[0], peak, q_weight, k_weight = lax.optimization_barrier((step[0], peak, q_weight, k_weight))
+    step = finish(mine, pieces + other)
     step = trade_planes(step, -1)
-    peak = peak[0, : max_logits.shape[1]]
-
-    gamma = jnp.minimum(1.0, clip_limit / peak)
-    root = jnp.sqrt(gamma)
-    local_heads = k_weight.shape[1] // NOPE
-    first_head = lax.axis_index("z") * local_heads
-    gamma_mine = lax.dynamic_slice_in_dim(gamma, first_head, local_heads)
-    root_mine = lax.dynamic_slice_in_dim(root, first_head, local_heads)
-    q_factor = jnp.concatenate(
-        [
-            jnp.broadcast_to(root_mine[:, None], (local_heads, NOPE)),
-            jnp.broadcast_to(gamma_mine[:, None], (local_heads, ROPE)),
-        ],
-        axis=1,
-    )
-    q_view = q_weight.reshape(q_weight.shape[0], local_heads, NOPE + ROPE).astype(jnp.float32)
-    q_clipped = (q_view * q_factor[None]).astype(jnp.bfloat16).reshape(q_weight.shape)
-    k_view = k_weight.reshape(k_weight.shape[0], local_heads, NOPE).astype(jnp.float32)
-    k_clipped = (k_view * root_mine[None, :, None]).astype(jnp.bfloat16).reshape(k_weight.shape)
-    step[0], q_clipped, k_clipped = lax.optimization_barrier((step[0], q_clipped, k_clipped))
-    step = jnp.swapaxes(spread_step(place, step, grads.shape[0]), 0, 1)
-    new_momentum = jnp.swapaxes(new_momentum, 0, 1)
-    return (new_momentum, step, q_clipped, k_clipped)
+    step = jnp.swapaxes(spread_step(step, grads.shape[0]), 0, 1)
+    return (jnp.swapaxes(new_momentum, 0, 1), step, q_clipped, k_clipped)
 
 
 def solution(mesh):

time: 151 us -> 140 us (0.927)
  local copies, waits for them, and re-layouts: 5.75 us -> 0.66 us
  Pallas kernels: 20.5 us -> 16.3 us
  other arithmetic: 3.07 us -> 0 us
  waiting for transfers between devices: 68.1 us -> 71 us
    unnamed x16 -> x8, local copies, waits for them, and re-layouts: 5.39 us -> 0.66 us
    convert_element_type x2 -> x0, other arithmetic: 2.98 us -> none  [the longest x1 1.6 us: body(): (q_view * q_factor[None]).astype(jnp.bfloat16).reshape(q_weight.shape)]
    ppermute x14, waiting for transfers between devices: 25 us -> 27.6 us  [trade_planes(): lax.ppermute(blocks[d], 'z', [(i, (i + sign * d) % NZ) for i in range(NZ)])]
    pallas_call x1, Pallas kernels: 3.35 us -> 1.8 us  [gram_band(): pl.pallas_call(gram_kernel, out_shape=[jax.ShapeDtypeStruct((QUARTER + EX...]
  transfers between devices with their start and end apart: 36 -> 36, of which waited for: 24 -> 24; matrix products, arithmetic and copies ran while one was open for 2% -> 0% of each run, Pallas kernels for 2% -> 3%
where the time goes in v1:
time: 140 us
  waiting for transfers between devices  71 us (51%)
  starting transfers between devices  51.2 us (37%)
  Pallas kernels  16.3 us (12%)
    ppermute x14, starting transfers between devices, trade_planes(): lax.ppermute(blocks[d], 'z', [(i, (i + sign * d) % NZ) for i in range(NZ)])  34.9 us
    ppermute x14, waiting for transfers between devices, trade_planes(): lax.ppermute(blocks[d], 'z', [(i, (i + sign * d) % NZ) for i in range(NZ)])  27.6 us
    ppermute x6, waiting for transfers between devices, send_along(): lax.ppermute(value, PLANE, permutation(lambda along, across: ((along + by...  26 us
    ppermute x4, waiting for transfers between devices, trade_across(): lax.ppermute(value, PLANE, permutation(lambda along, across, link=link: (...  13.2 us
    ppermute x6, starting transfers between devices, send_along(): lax.ppermute(value, PLANE, permutation(lambda along, across: ((along + by...  8.11 us
    pallas_call x1, Pallas kernels, finish(): pl.pallas_call(step_kernel, out_shape=[jax.ShapeDtypeStruct((16, PACKED),...  6.92 us
    ppermute x4, starting transfers between devices, trade_across(): lax.ppermute(value, PLANE, permutation(lambda along, across, link=link: (...  6.13 us
    ppermute x12, waiting for transfers between devices, swap_cores(): return lax.ppermute(value, 'c', [(0, 1), (1, 0)])  4.16 us
  transfers between devices with their start and end apart: 36, of which 24 were waited for; matrix products, arithmetic and copies ran while one was open for 0% of the time, Pallas kernels for 3%

profile of v1, /device:TPU:2, one launch (start us, length us, event | category | flops | bytes accessed | tf_op | source)
XLA Modules:
  0.0 140.0 jit_solution(11144328678286491394)
XLA Ops:
  1.3 2.2 %find_direction.1 = (bf16[16,3712]{1,0:T(8,128)(2,1)S(1)}, bf16[16,3712]{1,0:T(8,128)(2,1)S(1)}, bf16[16,3712]{1,0:T(8,128)(2,1)S(1)}, bf16[16,3712]{1,0:T(8,128...) custom-call(f32[1,64]{1,0:T(1,128)S(1)} %copy-done.3, ...), custom_call_target="tpu_custom_call" | custom-call | tf_op jit(solution)/shard_map/find_direction/pallas_call | solution.py:136
  3.5 2.0 %collective-permute-start = (bf16[16,3712]{1,0:T(8,128)(2,1)S(1)}, bf16[16,3712]{1,0:T(8,128)(2,1)S(1)}, u32[]{:S(2)}, u32[]{:S(2)}) collective-permute-start(bf16[16,3712]{1,0:T(8,128)(2,1)S(1)} %get-tuple-element.43), channel_id=1, source_target_pairs={{0,1},{1,2},{2,3},{3,4},{4,5},{5,6},{6,7},{7,0},{8,9},{9,10},{10,1... | collective-permute-start | bytes 356360 | tf_op jit(solution)/shard_map/ppermute | solution.py:482
  5.5 3.3 %collective-permute-start.1 = (bf16[16,3712]{1,0:T(8,128)(2,1)S(1)}, bf16[16,3712]{1,0:T(8,128)(2,1)S(1)}, u32[]{:S(2)}, u32[]{:S(2)}) collective-permute-start(bf16[16,3712]{1,0:T(8,128)(2,1)S(1)} %get-tuple-element.44), channel_id=1, source_target_pairs={{0,2},{1,3},{2,4},{3,5},{4,6},{5,7},{6,0},{7,1},{8,10},{9,11},{10,... | collective-permute-start | bytes 356360 | tf_op jit(solution)/shard_map/ppermute | solution.py:482
  8.8 4.0 %collective-permute-start.2 = (bf16[16,3712]{1,0:T(8,128)(2,1)S(1)}, bf16[16,3712]{1,0:T(8,128)(2,1)S(1)}, u32[]{:S(2)}, u32[]{:S(2)}) collective-permute-start(bf16[16,3712]{1,0:T(8,128)(2,1)S(1)} %get-tuple-element.45), channel_id=1, source_target_pairs={{0,3},{1,4},{2,5},{3,6},{4,7},{5,0},{6,1},{7,2},{8,11},{9,12},{10,... | collective-permute-start | bytes 356360 | tf_op jit(solution)/shard_map/ppermute | solution.py:482
  13.3 4.9 %collective-permute-start.4 = (bf16[16,3712]{1,0:T(8,128)(2,1)S(1)}, bf16[16,3712]{1,0:T(8,128)(2,1)S(1)}, u32[]{:S(2)}, u32[]{:S(2)}) collective-permute-start(bf16[16,3712]{1,0:T(8,128)(2,1)S(1)} %get-tuple-element.47), channel_id=1, source_target_pairs={{0,5},{1,6},{2,7},{3,0},{4,1},{5,2},{6,3},{7,4},{8,13},{9,14},{10,... | collective-permute-start | bytes 356360 | tf_op jit(solution)/shard_map/ppermute | solution.py:482
  18.3 2.7 %collective-permute-start.5 = (bf16[16,3712]{1,0:T(8,128)(2,1)S(1)}, bf16[16,3712]{1,0:T(8,128)(2,1)S(1)}, u32[]{:S(2)}, u32[]{:S(2)}) collective-permute-start(bf16[16,3712]{1,0:T(8,128)(2,1)S(1)} %get-tuple-element.48), channel_id=1, source_target_pairs={{0,6},{1,7},{2,0},{3,1},{4,2},{5,3},{6,4},{7,5},{8,14},{9,15},{10,... | collective-permute-start | bytes 356360 | tf_op jit(solution)/shard_map/ppermute | solution.py:482
  21.5 3.2 %collective-permute-start.6 = (bf16[16,3712]{1,0:T(8,128)(2,1)S(1)}, bf16[16,3712]{1,0:T(8,128)(2,1)S(1)}, u32[]{:S(2)}, u32[]{:S(2)}) collective-permute-start(bf16[16,3712]{1,0:T(8,128)(2,1)S(1)} %get-tuple-element.49), channel_id=1, source_target_pairs={{0,7},{1,0},{2,1},{3,2},{4,3},{5,4},{6,5},{7,6},{8,15},{9,8},{10,9... | collective-permute-start | bytes 356360 | tf_op jit(solution)/shard_map/ppermute | solution.py:482
  24.7 4.1 %collective-permute-done.2.refs_3_ = bf16[16,3712]{1,0:T(8,128)(2,1)S(1)} collective-permute-done((bf16[16,3712]{1,0:T(8,128)(2,1)S(1)}, bf16[16,3712]{1,0:T(8,128)(2,1)S(1)}, u32[]{:S(2)}, u32[]{:S(2)}) %collective-permute-start.2) | collective-permute-done | bytes 118816 | tf_op jit(solution)/shard_map/ppermute | solution.py:482
  29.4 3.7 %collective-permute-done.4.refs_5_ = bf16[16,3712]{1,0:T(8,128)(2,1)S(1)} collective-permute-done((bf16[16,3712]{1,0:T(8,128)(2,1)S(1)}, bf16[16,3712]{1,0:T(8,128)(2,1)S(1)}, u32[]{:S(2)}, u32[]{:S(2)}) %collective-permute-start.4) | collective-permute-done | bytes 118816 | tf_op jit(solution)/shard_map/ppermute | solution.py:482
  33.1 1.7 %collective-permute-done.5.refs_6_ = bf16[16,3712]{1,0:T(8,128)(2,1)S(1)} collective-permute-done((bf16[16,3712]{1,0:T(8,128)(2,1)S(1)}, bf16[16,3712]{1,0:T(8,128)(2,1)S(1)}, u32[]{:S(2)}, u32[]{:S(2)}) %collective-permute-start.5) | collective-permute-done | bytes 118816 | tf_op jit(solution)/shard_map/ppermute | solution.py:482
  37.9 1.8 %gram_band.1 = (bf16[272,1152]{1,0:T(8,128)(2,1)S(1)}, bf16[272,1152]{1,0:T(8,128)(2,1)S(1)}, bf16[272,1152]{1,0:T(8,128)(2,1)S(1)}, bf16[272,1152]{1,0:T(8,128)(2,1)S(1)}, bf16[256,2048]{1,0:T(8,128)(2,1)S(1)}) custom-call(bf16[16,3712]{1,0:T(8,128)(2,1)S(1)} %get-tuple-element.42.refs_0_, bf16[16,3712]{1,0:T(8,128)(2,1)S(1)} %collective-permute-done.refs_1_, ...), custom_call_target="tpu_custom_call" | custom-call | tf_op jit(solution)/shard_map/gram_band/pallas_call | solution.py:268
  39.7 1.7 %collective-permute-start.15 = (bf16[272,1152]{1,0:T(8,128)(2,1)S(1)}, bf16[272,1152]{1,0:T(8,128)(2,1)S(1)}, u32[]{:S(2)}, u32[]{:S(2)}) collective-permute-start(bf16[272,1152]{1,0:T(8,128)(2,1)S(1)} %get-tuple-element.57), channel_id=1, source_target_pairs={{0,64},{8,24},{16,80},{24,40},{32,96},{40,56},{48,112},{56,8},{64,... | collective-permute-start | bytes 1880072 | tf_op jit(solution)/shard_map/ppermute | solution.py:456
  42.6 2.2 %collective-permute-start.17 = (bf16[272,1152]{1,0:T(8,128)(2,1)S(1)}, bf16[272,1152]{1,0:T(8,128)(2,1)S(1)}, u32[]{:S(2)}, u32[]{:S(2)}) collective-permute-start(bf16[272,1152]{1,0:T(8,128)(2,1)S(1)} %get-tuple-element.59), channel_id=1, source_target_pairs={{0,192},{8,56},{16,208},{24,8},{32,224},{40,24},{48,240},{56,40},{... | collective-permute-start | bytes 1880072 | tf_op jit(solution)/shard_map/ppermute | solution.py:456
  44.7 2.4 %add_momentum.1 = f32[28,8,2048]{2,1,0:T(8,128)} custom-call(bf16[28,8,2048]{2,1,0:T(8,128)(2,1)S(1)} %bitcast.5, f32[28,8,2048]{2,1,0:T(8,128)} %bitcast.7), custom_call_target="tpu_custom_call" | custom-call | tf_op jit(solution)/shard_map/add_momentum/pallas_call | solution.py:177
  47.1 3.1 %collective-permute-done.15.refs_1_ = bf16[272,1152]{1,0:T(8,128)(2,1)S(1)} collective-permute-done((bf16[272,1152]{1,0:T(8,128)(2,1)S(1)}, bf16[272,1152]{1,0:T(8,128)(2,1)S(1)}, u32[]{:S(2)}, u32[]{:S(2)}) %collective-permute-start.15) | collective-permute-done | bytes 626720 | tf_op jit(solution)/shard_map/ppermute | solution.py:456
  50.3 3.1 %collective-permute-done.16.refs_2_ = bf16[272,1152]{1,0:T(8,128)(2,1)S(1)} collective-permute-done((bf16[272,1152]{1,0:T(8,128)(2,1)S(1)}, bf16[272,1152]{1,0:T(8,128)(2,1)S(1)}, u32[]{:S(2)}, u32[]{:S(2)}) %collective-permute-start.16) | collective-permute-done | bytes 626720 | tf_op jit(solution)/shard_map/ppermute | solution.py:456
  53.4 6.2 %collective-permute-done.17.refs_3_ = bf16[272,1152]{1,0:T(8,128)(2,1)S(1)} collective-permute-done((bf16[272,1152]{1,0:T(8,128)(2,1)S(1)}, bf16[272,1152]{1,0:T(8,128)(2,1)S(1)}, u32[]{:S(2)}, u32[]{:S(2)}) %collective-permute-start.17) | collective-permute-done | bytes 626720 | tf_op jit(solution)/shard_map/ppermute | solution.py:456
  61.6 2.2 %collective-permute-start.19 = (bf16[128,1152]{1,0:T(8,128)(2,1)S(1)}, bf16[128,1152]{1,0:T(8,128)(2,1)S(1)}, u32[]{:S(2)}, u32[]{:S(2)}) collective-permute-start(bf16[128,1152]{1,0:T(8,128)(2,1)S(1)} %get-tuple-element.61.refs_1_), channel_id=1, source_target_pairs={{0,48},{8,200},{16,32},{24,216},{32,16},{40,232},{48,0},{56,248},{... | collective-permute-start | bytes 884744 | tf_op jit(solution)/shard_map/ppermute | solution.py:465
  63.8 5.7 %collective-permute-done.19.refs_3_ = bf16[128,1152]{1,0:T(8,128)(2,1)S(1)} collective-permute-done((bf16[128,1152]{1,0:T(8,128)(2,1)S(1)}, bf16[128,1152]{1,0:T(8,128)(2,1)S(1)}, u32[]{:S(2)}, u32[]{:S(2)}) %collective-permute-start.19) | collective-permute-done | bytes 294944 | tf_op jit(solution)/shard_map/ppermute | solution.py:465
  69.7 2.3 %collective-permute-start.20 = (bf16[144,1152]{1,0:T(8,128)(2,1)S(1)}, bf16[144,1152]{1,0:T(8,128)(2,1)S(1)}, u32[]{:S(2)}, u32[]{:S(2)}) collective-permute-start(bf16[144,1152]{1,0:T(8,128)(2,1)S(1)} %get-tuple-element.62.refs_0_), channel_id=1, source_target_pairs={{0,48},{8,200},{16,32},{24,216},{32,16},{40,232},{48,0},{56,248},{... | collective-permute-start | bytes 995336 | tf_op jit(solution)/shard_map/ppermute | solution.py:465
  71.9 7.5 %collective-permute-done.21.refs_3_ = bf16[128,1152]{1,0:T(8,128)(2,1)S(1)} collective-permute-done((bf16[128,1152]{1,0:T(8,128)(2,1)S(1)}, bf16[128,1152]{1,0:T(8,128)(2,1)S(1)}, u32[]{:S(2)}, u32[]{:S(2)}) %collective-permute-start.21) | collective-permute-done | bytes 294944 | tf_op jit(solution)/shard_map/ppermute | solution.py:465
  83.8 5.7 %collective-permute-done.22.refs_1_ = bf16[256,1152]{1,0:T(8,128)(2,1)S(1)} collective-permute-done((bf16[256,1152]{1,0:T(8,128)(2,1)S(1)}, bf16[256,1152]{1,0:T(8,128)(2,1)S(1)}, u32[]{:S(2)}, u32[]{:S(2)}) %collective-permute-start.22) | collective-permute-done | bytes 589856 | tf_op jit(solution)/shard_map/ppermute | solution.py:456
  89.5 7.8 %collective-permute-done.24.refs_3_ = bf16[256,1152]{1,0:T(8,128)(2,1)S(1)} collective-permute-done((bf16[256,1152]{1,0:T(8,128)(2,1)S(1)}, bf16[256,1152]{1,0:T(8,128)(2,1)S(1)}, u32[]{:S(2)}, u32[]{:S(2)}) %collective-permute-start.24) | collective-permute-done | bytes 589856 | tf_op jit(solution)/shard_map/ppermute | solution.py:456
  101.0 6.9 %finish.1 = (bf16[16,3584]{1,0:T(8,128)(2,1)S(1)}, bf16[16,3584]{1,0:T(8,128)(2,1)S(1)}, bf16[16,3584]{1,0:T(8,128)(2,1)S(1)}, bf16[16,3584]{1,0:T(8,128)(2,1)S(...) custom-call(bf16[256,2048]{1,0:T(8,128)(2,1)S(1)} %get-tuple-element, ...), custom_call_target="tpu_custom_call" | custom-call | tf_op jit(solution)/shard_map/finish/pallas_call | solution.py:395
  108.0 2.7 %collective-permute-start.29 = (bf16[16,3584]{1,0:T(8,128)(2,1)S(1)}, bf16[16,3584]{1,0:T(8,128)(2,1)S(1)}, u32[]{:S(2)}, u32[]{:S(2)}) collective-permute-start(bf16[16,3584]{1,0:T(8,128)(2,1)S(1)} %get-tuple-element.71), channel_id=1, source_target_pairs={{0,7},{1,0},{2,1},{3,2},{4,3},{5,4},{6,5},{7,6},{8,15},{9,8},{10,9... | collective-permute-start | bytes 344072 | tf_op jit(solution)/shard_map/ppermute | solution.py:482
  111.2 3.8 %collective-permute-start.31 = (bf16[16,3584]{1,0:T(8,128)(2,1)S(1)}, bf16[16,3584]{1,0:T(8,128)(2,1)S(1)}, u32[]{:S(2)}, u32[]{:S(2)}) collective-permute-start(bf16[16,3584]{1,0:T(8,128)(2,1)S(1)} %get-tuple-element.73), channel_id=1, source_target_pairs={{0,5},{1,6},{2,7},{3,0},{4,1},{5,2},{6,3},{7,4},{8,13},{9,14},{10,... | collective-permute-start | bytes 344072 | tf_op jit(solution)/shard_map/ppermute | solution.py:482
  116.7 3.0 %collective-permute-start.33 = (bf16[16,3584]{1,0:T(8,128)(2,1)S(1)}, bf16[16,3584]{1,0:T(8,128)(2,1)S(1)}, u32[]{:S(2)}, u32[]{:S(2)}) collective-permute-start(bf16[16,3584]{1,0:T(8,128)(2,1)S(1)} %get-tuple-element.75), channel_id=1, source_target_pairs={{0,3},{1,4},{2,5},{3,6},{4,7},{5,0},{6,1},{7,2},{8,11},{9,12},{10,... | collective-permute-start | bytes 344072 | tf_op jit(solution)/shard_map/ppermute | solution.py:482
  119.8 2.4 %collective-permute-start.34 = (bf16[16,3584]{1,0:T(8,128)(2,1)S(1)}, bf16[16,3584]{1,0:T(8,128)(2,1)S(1)}, u32[]{:S(2)}, u32[]{:S(2)}) collective-permute-start(bf16[16,3584]{1,0:T(8,128)(2,1)S(1)} %get-tuple-element.76), channel_id=1, source_target_pairs={{0,2},{1,3},{2,4},{3,5},{4,6},{5,7},{6,0},{7,1},{8,10},{9,11},{10,... | collective-permute-start | bytes 344072 | tf_op jit(solution)/shard_map/ppermute | solution.py:482
  122.2 3.4 %collective-permute-done.30.refs_2_ = bf16[16,3584]{1,0:T(8,128)(2,1)S(1)} collective-permute-done((bf16[16,3584]{1,0:T(8,128)(2,1)S(1)}, bf16[16,3584]{1,0:T(8,128)(2,1)S(1)}, u32[]{:S(2)}, u32[]{:S(2)}) %collective-permute-start.30) | collective-permute-done | bytes 114720 | tf_op jit(solution)/shard_map/ppermute | solution.py:482
  125.6 3.1 %collective-permute-done.32.refs_4_ = bf16[16,3584]{1,0:T(8,128)(2,1)S(1)} collective-permute-done((bf16[16,3584]{1,0:T(8,128)(2,1)S(1)}, bf16[16,3584]{1,0:T(8,128)(2,1)S(1)}, u32[]{:S(2)}, u32[]{:S(2)}) %collective-permute-start.32) | collective-permute-done | bytes 114720 | tf_op jit(solution)/shard_map/ppermute | solution.py:482
  128.7 6.0 %collective-permute-done.33.refs_5_ = bf16[16,3584]{1,0:T(8,128)(2,1)S(1)} collective-permute-done((bf16[16,3584]{1,0:T(8,128)(2,1)S(1)}, bf16[16,3584]{1,0:T(8,128)(2,1)S(1)}, u32[]{:S(2)}, u32[]{:S(2)}) %collective-permute-start.33) | collective-permute-done | bytes 114720 | tf_op jit(solution)/shard_map/ppermute | solution.py:482
  134.7 3.9 %collective-permute-done.35.refs_7_ = bf16[16,3584]{1,0:T(8,128)(2,1)S(1)} collective-permute-done((bf16[16,3584]{1,0:T(8,128)(2,1)S(1)}, bf16[16,3584]{1,0:T(8,128)(2,1)S(1)}, u32[]{:S(2)}, u32[]{:S(2)}) %collective-permute-start.35) | collective-permute-done | bytes 114720 | tf_op jit(solution)/shard_map/ppermute | solution.py:482
  (57 shorter events, 20.2 us)
Async XLA Ops:
  3.5 14.8 %collective-permute-start = (bf16[16,3712]{1,0:T(8,128)(2,1)S(1)}, bf16[16,3712]{1,0:T(8,128)(2,1)S(1)}, u32[]{:S(2)}, u32[]{:S(2)}) collective-permute-start(bf16[16,3712]{1,0:T(8,128)(2,1)S(1)} %get-tuple-element.43), channel_id=1, source_target_pairs={{0,1},{1,2},{2,3},{3,4},{4,5},{5,6},{6,7},{7,0},{8,9},{9,10},{10,1... | collective-permute-start | bytes 356360 | tf_op jit(solution)/shard_map/ppermute | solution.py:482
  5.5 16.0 %collective-permute-start.1 = (bf16[16,3712]{1,0:T(8,128)(2,1)S(1)}, bf16[16,3712]{1,0:T(8,128)(2,1)S(1)}, u32[]{:S(2)}, u32[]{:S(2)}) collective-permute-start(bf16[16,3712]{1,0:T(8,128)(2,1)S(1)} %get-tuple-element.44), channel_id=1, source_target_pairs={{0,2},{1,3},{2,4},{3,5},{4,6},{5,7},{6,0},{7,1},{8,10},{9,11},{10,... | collective-permute-start | bytes 356360 | tf_op jit(solution)/shard_map/ppermute | solution.py:482
  8.8 20.1 %collective-permute-start.2 = (bf16[16,3712]{1,0:T(8,128)(2,1)S(1)}, bf16[16,3712]{1,0:T(8,128)(2,1)S(1)}, u32[]{:S(2)}, u32[]{:S(2)}) collective-permute-start(bf16[16,3712]{1,0:T(8,128)(2,1)S(1)} %get-tuple-element.45), channel_id=1, source_target_pairs={{0,3},{1,4},{2,5},{3,6},{4,7},{5,0},{6,1},{7,2},{8,11},{9,12},{10,... | collective-permute-start | bytes 356360 | tf_op jit(solution)/shard_map/ppermute | solution.py:482
  12.8 16.1 %collective-permute-start.3 = (bf16[16,3712]{1,0:T(8,128)(2,1)S(1)}, bf16[16,3712]{1,0:T(8,128)(2,1)S(1)}, u32[]{:S(2)}, u32[]{:S(2)}) collective-permute-start(bf16[16,3712]{1,0:T(8,128)(2,1)S(1)} %get-tuple-element.46), channel_id=1, source_target_pairs={{0,4},{1,5},{2,6},{3,7},{4,0},{5,1},{6,2},{7,3},{8,12},{9,13},{10,... | collective-permute-start | bytes 356360 | tf_op jit(solution)/shard_map/ppermute | solution.py:482
  13.3 19.7 %collective-permute-start.4 = (bf16[16,3712]{1,0:T(8,128)(2,1)S(1)}, bf16[16,3712]{1,0:T(8,128)(2,1)S(1)}, u32[]{:S(2)}, u32[]{:S(2)}) collective-permute-start(bf16[16,3712]{1,0:T(8,128)(2,1)S(1)} %get-tuple-element.47), channel_id=1, source_target_pairs={{0,5},{1,6},{2,7},{3,0},{4,1},{5,2},{6,3},{7,4},{8,13},{9,14},{10,... | collective-permute-start | bytes 356360 | tf_op jit(solution)/shard_map/ppermute | solution.py:482
  18.3 16.5 %collective-permute-start.5 = (bf16[16,3712]{1,0:T(8,128)(2,1)S(1)}, bf16[16,3712]{1,0:T(8,128)(2,1)S(1)}, u32[]{:S(2)}, u32[]{:S(2)}) collective-permute-start(bf16[16,3712]{1,0:T(8,128)(2,1)S(1)} %get-tuple-element.48), channel_id=1, source_target_pairs={{0,6},{1,7},{2,0},{3,1},{4,2},{5,3},{6,4},{7,5},{8,14},{9,15},{10,... | collective-permute-start | bytes 356360 | tf_op jit(solution)/shard_map/ppermute | solution.py:482
  21.5 14.4 %collective-permute-start.6 = (bf16[16,3712]{1,0:T(8,128)(2,1)S(1)}, bf16[16,3712]{1,0:T(8,128)(2,1)S(1)}, u32[]{:S(2)}, u32[]{:S(2)}) collective-permute-start(bf16[16,3712]{1,0:T(8,128)(2,1)S(1)} %get-tuple-element.49), channel_id=1, source_target_pairs={{0,7},{1,0},{2,1},{3,2},{4,3},{5,4},{6,5},{7,6},{8,15},{9,8},{10,9... | collective-permute-start | bytes 356360 | tf_op jit(solution)/shard_map/ppermute | solution.py:482
  28.8 7.0 %collective-permute-start.7 = (bf16[16,3712]{1,0:T(8,128)(2,1)S(1)}, bf16[16,3712]{1,0:T(8,128)(2,1)S(1)}, u32[]{:S(2)}, u32[]{:S(2)}) collective-permute-start(bf16[16,3712]{1,0:T(8,128)(2,1)S(1)} %get-tuple-element.42.refs_0_), channel_id=1, source_target_pairs={{0,8},{8,0},{1,9},{9,1},{2,10},{10,2},{3,11},{11,3},{4,12},{12,4},... | collective-permute-start | bytes 356360 | tf_op jit(solution)/shard_map/ppermute | solution.py:476
  28.9 7.6 %collective-permute-start.8 = (bf16[16,3712]{1,0:T(8,128)(2,1)S(1)}, bf16[16,3712]{1,0:T(8,128)(2,1)S(1)}, u32[]{:S(2)}, u32[]{:S(2)}) collective-permute-start(bf16[16,3712]{1,0:T(8,128)(2,1)S(1)} %collective-permute-done.refs_1_), channel_id=1, source_target_pairs={{0,8},{8,0},{1,9},{9,1},{2,10},{10,2},{3,11},{11,3},{4,12},{12,4},... | collective-permute-start | bytes 356360 | tf_op jit(solution)/shard_map/ppermute | solution.py:476
  33.1 3.4 %collective-permute-start.9 = (bf16[16,3712]{1,0:T(8,128)(2,1)S(1)}, bf16[16,3712]{1,0:T(8,128)(2,1)S(1)}, u32[]{:S(2)}, u32[]{:S(2)}) collective-permute-start(bf16[16,3712]{1,0:T(8,128)(2,1)S(1)} %collective-permute-done.1.refs_2_), channel_id=1, source_target_pairs={{0,8},{8,0},{1,9},{9,1},{2,10},{10,2},{3,11},{11,3},{4,12},{12,4},... | collective-permute-start | bytes 356360 | tf_op jit(solution)/shard_map/ppermute | solution.py:476
  34.8 2.1 %collective-permute-start.10 = (bf16[16,3712]{1,0:T(8,128)(2,1)S(1)}, bf16[16,3712]{1,0:T(8,128)(2,1)S(1)}, u32[]{:S(2)}, u32[]{:S(2)}) collective-permute-start(bf16[16,3712]{1,0:T(8,128)(2,1)S(1)} %collective-permute-done.2.refs_3_), channel_id=1, source_target_pairs={{0,8},{8,0},{1,9},{9,1},{2,10},{10,2},{3,11},{11,3},{4,12},{12,4},... | collective-permute-start | bytes 356360 | tf_op jit(solution)/shard_map/ppermute | solution.py:476
  39.7 10.5 %collective-permute-start.15 = (bf16[272,1152]{1,0:T(8,128)(2,1)S(1)}, bf16[272,1152]{1,0:T(8,128)(2,1)S(1)}, u32[]{:S(2)}, u32[]{:S(2)}) collective-permute-start(bf16[272,1152]{1,0:T(8,128)(2,1)S(1)} %get-tuple-element.57), channel_id=1, source_target_pairs={{0,64},{8,24},{16,80},{24,40},{32,96},{40,56},{48,112},{56,8},{64,... | collective-permute-start | bytes 1880072 | tf_op jit(solution)/shard_map/ppermute | solution.py:456
  41.5 11.9 %collective-permute-start.16 = (bf16[272,1152]{1,0:T(8,128)(2,1)S(1)}, bf16[272,1152]{1,0:T(8,128)(2,1)S(1)}, u32[]{:S(2)}, u32[]{:S(2)}) collective-permute-start(bf16[272,1152]{1,0:T(8,128)(2,1)S(1)} %get-tuple-element.58), channel_id=1, source_target_pairs={{0,128},{8,40},{16,144},{24,56},{32,160},{40,8},{48,176},{56,24},{... | collective-permute-start | bytes 1880072 | tf_op jit(solution)/shard_map/ppermute | solution.py:456
  42.6 17.0 %collective-permute-start.17 = (bf16[272,1152]{1,0:T(8,128)(2,1)S(1)}, bf16[272,1152]{1,0:T(8,128)(2,1)S(1)}, u32[]{:S(2)}, u32[]{:S(2)}) collective-permute-start(bf16[272,1152]{1,0:T(8,128)(2,1)S(1)} %get-tuple-element.59), channel_id=1, source_target_pairs={{0,192},{8,56},{16,208},{24,8},{32,224},{40,24},{48,240},{56,40},{... | collective-permute-start | bytes 1880072 | tf_op jit(solution)/shard_map/ppermute | solution.py:456
  59.9 9.6 %collective-permute-start.18 = (bf16[144,1152]{1,0:T(8,128)(2,1)S(1)}, bf16[144,1152]{1,0:T(8,128)(2,1)S(1)}, u32[]{:S(2)}, u32[]{:S(2)}) collective-permute-start(bf16[144,1152]{1,0:T(8,128)(2,1)S(1)} %get-tuple-element.60.refs_0_), channel_id=1, source_target_pairs={{0,16},{8,72},{16,0},{24,88},{32,48},{40,104},{48,32},{56,120},{64... | collective-permute-start | bytes 995336 | tf_op jit(solution)/shard_map/ppermute | solution.py:465
  61.6 7.9 %collective-permute-start.19 = (bf16[128,1152]{1,0:T(8,128)(2,1)S(1)}, bf16[128,1152]{1,0:T(8,128)(2,1)S(1)}, u32[]{:S(2)}, u32[]{:S(2)}) collective-permute-start(bf16[128,1152]{1,0:T(8,128)(2,1)S(1)} %get-tuple-element.61.refs_1_), channel_id=1, source_target_pairs={{0,48},{8,200},{16,32},{24,216},{32,16},{40,232},{48,0},{56,248},{... | collective-permute-start | bytes 884744 | tf_op jit(solution)/shard_map/ppermute | solution.py:465
  69.7 9.8 %collective-permute-start.20 = (bf16[144,1152]{1,0:T(8,128)(2,1)S(1)}, bf16[144,1152]{1,0:T(8,128)(2,1)S(1)}, u32[]{:S(2)}, u32[]{:S(2)}) collective-permute-start(bf16[144,1152]{1,0:T(8,128)(2,1)S(1)} %get-tuple-element.62.refs_0_), channel_id=1, source_target_pairs={{0,48},{8,200},{16,32},{24,216},{32,16},{40,232},{48,0},{56,248},{... | collective-permute-start | bytes 995336 | tf_op jit(solution)/shard_map/ppermute | solution.py:465
  71.9 7.5 %collective-permute-start.21 = (bf16[128,1152]{1,0:T(8,128)(2,1)S(1)}, bf16[128,1152]{1,0:T(8,128)(2,1)S(1)}, u32[]{:S(2)}, u32[]{:S(2)}) collective-permute-start(bf16[128,1152]{1,0:T(8,128)(2,1)S(1)} %get-tuple-element.63.refs_1_), channel_id=1, source_target_pairs={{0,16},{8,72},{16,0},{24,88},{32,48},{40,104},{48,32},{56,120},{64... | collective-permute-start | bytes 884744 | tf_op jit(solution)/shard_map/ppermute | solution.py:465
  79.6 10.0 %collective-permute-start.22 = (bf16[256,1152]{1,0:T(8,128)(2,1)S(1)}, bf16[256,1152]{1,0:T(8,128)(2,1)S(1)}, u32[]{:S(2)}, u32[]{:S(2)}) collective-permute-start(bf16[256,1152]{1,0:T(8,128)(2,1)S(1)} %get-tuple-element.68.refs_0_), channel_id=1, source_target_pairs={{0,64},{8,24},{16,80},{24,40},{32,96},{40,56},{48,112},{56,8},{64,... | collective-permute-start | bytes 1769480 | tf_op jit(solution)/shard_map/ppermute | solution.py:456
  81.1 16.2 %collective-permute-start.24 = (bf16[256,1152]{1,0:T(8,128)(2,1)S(1)}, bf16[256,1152]{1,0:T(8,128)(2,1)S(1)}, u32[]{:S(2)}, u32[]{:S(2)}) collective-permute-start(bf16[256,1152]{1,0:T(8,128)(2,1)S(1)} %get-tuple-element.68.refs_0_), channel_id=1, source_target_pairs={{0,192},{8,56},{16,208},{24,8},{32,224},{40,24},{48,240},{56,40},{... | collective-permute-start | bytes 1769480 | tf_op jit(solution)/shard_map/ppermute | solution.py:456
  81.7 15.7 %collective-permute-start.23 = (bf16[256,1152]{1,0:T(8,128)(2,1)S(1)}, bf16[256,1152]{1,0:T(8,128)(2,1)S(1)}, u32[]{:S(2)}, u32[]{:S(2)}) collective-permute-start(bf16[256,1152]{1,0:T(8,128)(2,1)S(1)} %get-tuple-element.68.refs_0_), channel_id=1, source_target_pairs={{0,128},{8,40},{16,144},{24,56},{32,160},{40,8},{48,176},{56,24},{... | collective-permute-start | bytes 1769480 | tf_op jit(solution)/shard_map/ppermute | solution.py:456
  89.5 10.7 %collective-permute-start.25 = (bf16[256,1152]{1,0:T(8,128)(2,1)S(1)}, bf16[256,1152]{1,0:T(8,128)(2,1)S(1)}, u32[]{:S(2)}, u32[]{:S(2)}) collective-permute-start(bf16[256,1152]{1,0:T(8,128)(2,1)S(1)} %get-tuple-element.68.refs_0_), channel_id=1, source_target_pairs={{0,8},{8,0},{1,9},{9,1},{2,10},{10,2},{3,11},{11,3},{4,12},{12,4},... | collective-permute-start | bytes 1769480 | tf_op jit(solution)/shard_map/ppermute | solution.py:476
  97.3 2.0 %collective-permute-start.28 = (bf16[256,1152]{1,0:T(8,128)(2,1)S(1)}, bf16[256,1152]{1,0:T(8,128)(2,1)S(1)}, u32[]{:S(2)}, u32[]{:S(2)}) collective-permute-start(bf16[256,1152]{1,0:T(8,128)(2,1)S(1)} %collective-permute-done.24.refs_3_), channel_id=1, source_target_pairs={{0,8},{8,0},{1,9},{9,1},{2,10},{10,2},{3,11},{11,3},{4,12},{12,4},... | collective-permute-start | bytes 1769480 | tf_op jit(solution)/shard_map/ppermute | solution.py:476
  97.3 2.8 %collective-permute-start.27 = (bf16[256,1152]{1,0:T(8,128)(2,1)S(1)}, bf16[256,1152]{1,0:T(8,128)(2,1)S(1)}, u32[]{:S(2)}, u32[]{:S(2)}) collective-permute-start(bf16[256,1152]{1,0:T(8,128)(2,1)S(1)} %collective-permute-done.23.refs_2_), channel_id=1, source_target_pairs={{0,8},{8,0},{1,9},{9,1},{2,10},{10,2},{3,11},{11,3},{4,12},{12,4},... | collective-permute-start | bytes 1769480 | tf_op jit(solution)/shard_map/ppermute | solution.py:476
  97.9 3.2 %collective-permute-start.26 = (bf16[256,1152]{1,0:T(8,128)(2,1)S(1)}, bf16[256,1152]{1,0:T(8,128)(2,1)S(1)}, u32[]{:S(2)}, u32[]{:S(2)}) collective-permute-start(bf16[256,1152]{1,0:T(8,128)(2,1)S(1)} %collective-permute-done.22.refs_1_), channel_id=1, source_target_pairs={{0,8},{8,0},{1,9},{9,1},{2,10},{10,2},{3,11},{11,3},{4,12},{12,4},... | collective-permute-start | bytes 1769480 | tf_op jit(solution)/shard_map/ppermute | solution.py:476
  108.0 11.8 %collective-permute-start.29 = (bf16[16,3584]{1,0:T(8,128)(2,1)S(1)}, bf16[16,3584]{1,0:T(8,128)(2,1)S(1)}, u32[]{:S(2)}, u32[]{:S(2)}) collective-permute-start(bf16[16,3584]{1,0:T(8,128)(2,1)S(1)} %get-tuple-element.71), channel_id=1, source_target_pairs={{0,7},{1,0},{2,1},{3,2},{4,3},{5,4},{6,5},{7,6},{8,15},{9,8},{10,9... | collective-permute-start | bytes 344072 | tf_op jit(solution)/shard_map/ppermute | solution.py:482
  110.7 14.8 %collective-permute-start.30 = (bf16[16,3584]{1,0:T(8,128)(2,1)S(1)}, bf16[16,3584]{1,0:T(8,128)(2,1)S(1)}, u32[]{:S(2)}, u32[]{:S(2)}) collective-permute-start(bf16[16,3584]{1,0:T(8,128)(2,1)S(1)} %get-tuple-element.72), channel_id=1, source_target_pairs={{0,6},{1,7},{2,0},{3,1},{4,2},{5,3},{6,4},{7,5},{8,14},{9,15},{10,... | collective-permute-start | bytes 344072 | tf_op jit(solution)/shard_map/ppermute | solution.py:482
  111.2 14.4 %collective-permute-start.31 = (bf16[16,3584]{1,0:T(8,128)(2,1)S(1)}, bf16[16,3584]{1,0:T(8,128)(2,1)S(1)}, u32[]{:S(2)}, u32[]{:S(2)}) collective-permute-start(bf16[16,3584]{1,0:T(8,128)(2,1)S(1)} %get-tuple-element.73), channel_id=1, source_target_pairs={{0,5},{1,6},{2,7},{3,0},{4,1},{5,2},{6,3},{7,4},{8,13},{9,14},{10,... | collective-permute-start | bytes 344072 | tf_op jit(solution)/shard_map/ppermute | solution.py:482
  115.0 13.6 %collective-permute-start.32 = (bf16[16,3584]{1,0:T(8,128)(2,1)S(1)}, bf16[16,3584]{1,0:T(8,128)(2,1)S(1)}, u32[]{:S(2)}, u32[]{:S(2)}) collective-permute-start(bf16[16,3584]{1,0:T(8,128)(2,1)S(1)} %get-tuple-element.74), channel_id=1, source_target_pairs={{0,4},{1,5},{2,6},{3,7},{4,0},{5,1},{6,2},{7,3},{8,12},{9,13},{10,... | collective-permute-start | bytes 344072 | tf_op jit(solution)/shard_map/ppermute | solution.py:482
  116.7 17.9 %collective-permute-start.33 = (bf16[16,3584]{1,0:T(8,128)(2,1)S(1)}, bf16[16,3584]{1,0:T(8,128)(2,1)S(1)}, u32[]{:S(2)}, u32[]{:S(2)}) collective-permute-start(bf16[16,3584]{1,0:T(8,128)(2,1)S(1)} %get-tuple-element.75), channel_id=1, source_target_pairs={{0,3},{1,4},{2,5},{3,6},{4,7},{5,0},{6,1},{7,2},{8,11},{9,12},{10,... | collective-permute-start | bytes 344072 | tf_op jit(solution)/shard_map/ppermute | solution.py:482
  119.8 14.9 %collective-permute-start.34 = (bf16[16,3584]{1,0:T(8,128)(2,1)S(1)}, bf16[16,3584]{1,0:T(8,128)(2,1)S(1)}, u32[]{:S(2)}, u32[]{:S(2)}) collective-permute-start(bf16[16,3584]{1,0:T(8,128)(2,1)S(1)} %get-tuple-element.76), channel_id=1, source_target_pairs={{0,2},{1,3},{2,4},{3,5},{4,6},{5,7},{6,0},{7,1},{8,10},{9,11},{10,... | collective-permute-start | bytes 344072 | tf_op jit(solution)/shard_map/ppermute | solution.py:482
  125.5 13.1 %collective-permute-start.35 = (bf16[16,3584]{1,0:T(8,128)(2,1)S(1)}, bf16[16,3584]{1,0:T(8,128)(2,1)S(1)}, u32[]{:S(2)}, u32[]{:S(2)}) collective-permute-start(bf16[16,3584]{1,0:T(8,128)(2,1)S(1)} %get-tuple-element.77), channel_id=1, source_target_pairs={{0,1},{1,2},{2,3},{3,4},{4,5},{5,6},{6,7},{7,0},{8,9},{9,10},{10,1... | collective-permute-start | bytes 344072 | tf_op jit(solution)/shard_map/ppermute | solution.py:482
  (8 other events, 95.3 us)
